TPU v7x, 128 devices: a whole 4x4x4 slice. The times are simulated.
128 devices in a mesh: grp: 8 (over y, core), dev: 16 (over z, x).
Axes of the slice: x: 4, y: 4, z: 4, core: 2. Of those that a mesh axis runs over, the one named last changes fastest.
Arguments:
- slab: bfloat16 [262144, 4096], P(('grp', 'dev')), may hold values from -1000 to 1000
- sketch_map: bfloat16 [4096, 320], replicated, may hold values from -0.09375 to 0.09375
Outputs:
- basis: float32 [262144, 320], P(('grp', 'dev'))
- coeffs: float32 [320, 4096], P(None, 'dev')
All inputs are finite; a program needn't handle non-finite values.
Results may differ from a plain program's by a relative error of at most 0.0022.
Values sent between devices are 32-bit elements; how exact they have to be, the bound alone decides.
A program may use at most 128 MiB of HBM per device.

v0:
```python
import math

import jax
import jax.numpy as jnp
from jax import lax
from jax.sharding import PartitionSpec as P


def contract_rows(left, right):
    return lax.dot_general(
        left, right, (((0,), (0,)), ((), ())), preferred_element_type=jnp.float32
    )


def total_gram(local_gram):
    return lax.psum(local_gram, ("grp", "dev"))


def local(slab, sketch_map):
    rows = slab.shape[0] * lax.axis_size("grp") * lax.axis_size("dev")
    scale = math.sqrt(rows)
    sketch = jnp.dot(slab, sketch_map, preferred_element_type=jnp.float32)
    local_gram = jnp.dot(sketch.T, sketch, precision=lax.Precision.HIGHEST)
    sketch_high = sketch.astype(jnp.bfloat16)
    sketch_low = (sketch - sketch_high.astype(jnp.float32)).astype(jnp.bfloat16)
    width = slab.shape[1] // lax.axis_size("dev")
    cross = contract_rows(sketch_high, slab) + contract_rows(sketch_low, slab)
    gram = total_gram(local_gram)
    cross = lax.psum(cross, ("grp", "dev"))
    cross_local = lax.dynamic_slice_in_dim(cross, lax.axis_index("dev") * width, width, 1)
    lower = jnp.linalg.cholesky(gram)
    basis = lax.linalg.triangular_solve(lower, sketch.T, left_side=True, lower=True).T * scale
    coeffs = lax.linalg.triangular_solve(lower, cross_local, left_side=True, lower=True) / scale
    return (basis, coeffs)


def solution(mesh):
    in_specs = (P(("grp", "dev"), None), P())
    out_specs = (P(("grp", "dev"), None), P(None, "dev"))
    return jax.shard_map(local, mesh=mesh, in_specs=in_specs, out_specs=out_specs, check_vma=False)
```

profile of v0, /device:TPU:1, one launch (start us, length us, event | category | flops | bytes accessed | tf_op | source)
XLA Modules:
  0.0 317.8 jit_solution(5630332590232520842)
XLA Ops:
  7.2 1.7 copy-done
  8.9 11.0 %fusion.35 = f32[2048,320]{0,1:T(8,128)S(1)} fusion(bf16[2048,4096]{1,0:T(8,128)(2,1)} %param.2, bf16[4096,320]{0,1:T(8,128)(2,1)S(1)} %copy-done), kind=kOutput, calls=%fused_computation.74 | convolution fusion | flops 5368709120 | bytes 22020096 | tf_op jit(solution)/shard_map/dot_general | solution.py:22
  19.9 7.4 %fusion.7 = f32[320,4096]{1,0:T(8,128)} fusion(bf16[2048,4096]{1,0:T(8,128)(2,1)S(1)} %copy-done.6, f32[2048,320]{0,1:T(8,128)S(1)} %fusion.35), kind=kOutput, calls=%fused_computation.19 | convolution fusion | flops 5369364480 | bytes 24641536 | tf_op jit(solution)/shard_map/dot_general | solution.py:10
  27.4 5.1 %fusion.36 = f32[320,320]{0,1:T(8,128)} fusion(f32[2048,320]{0,1:T(8,128)S(1)} %fusion.35), kind=kOutput, calls=%fused_computation.75 | convolution fusion | flops 2516582400 | bytes 3031040 | tf_op jit(solution)/shard_map/dot_general | solution.py:23
  32.5 9.2 %convolution_add_fusion = f32[320,4096]{1,0:T(8,128)} fusion(f32[320,4096]{1,0:T(8,128)} %fusion.7, bf16[2048,4096]{1,0:T(8,128)(2,1)S(1)} %copy-done.6, f32[2048,320]{0,1:T(8,128)S(1)} %fusion.35), kind=kOutput, calls=%fused_computation.2 | convolution fusion | flops 5372641280 | bytes 29884416 | tf_op jit(solution)/shard_map/dot_general | solution.py:10
  41.8 160.7 %all-reduce.6.cloned.1.call-done = (f32[320,320]{0,1:T(8,128)}, f32[320,4096]{1,0:T(8,128)}) async-done(((f32[320,320]{0,1:T(8,128)}, f32[320,4096]{1,0:T(8,128)}), (f32[320,320]{0,1:T(8,128)}, f32[320,4096]{1,0:T(8,128)})) %all-reduce.6.cloned.1.call-update) | async-done | bytes 5652496 | tf_op jit(solution)/shard_map/psum | solution.py:16
  202.5 1.2 copy.5
  205.6 11.7 %cholesky.78 = f32[128,128]{1,0:T(8,128)S(1)} custom-call(f32[128,128]{1,0:T(8,128)S(1)} %cholesky.198), custom_call_target="Cholesky" | custom-call | tf_op jit(solution)/shard_map/jit(cholesky)/cholesky | solution.py:31
  217.4 9.8 %custom-call.24 = f32[1,128,128]{1,2,0:T(8,128)S(1)} custom-call(f32[1,128,128]{2,1,0:T(8,128)S(1)} %get-tuple-element.26), custom_call_target="InvertDiagBlocksLowerTriangular" | custom-call | tf_op jit(solution)/shard_map/jit(cholesky)/cholesky | solution.py:31
  227.2 1.1 constant_dynamic-update-slice_fusion.1
  228.3 1.2 convolution_subtract_fusion.3
  229.5 11.7 %cholesky.164 = f32[128,128]{1,0:T(8,128)S(1)} custom-call(f32[128,128]{1,0:T(8,128)S(1)} %cholesky.202), custom_call_target="Cholesky" | custom-call | tf_op jit(solution)/shard_map/jit(cholesky)/cholesky | solution.py:31
  241.3 10.0 %custom-call.25 = f32[1,128,128]{1,2,0:T(8,128)S(1)} custom-call(f32[1,128,128]{2,1,0:T(8,128)S(1)} %get-tuple-element.23), custom_call_target="InvertDiagBlocksLowerTriangular" | custom-call | tf_op jit(solution)/shard_map/jit(cholesky)/cholesky | solution.py:31
  252.4 5.8 %cholesky.186 = f32[64,64]{1,0:T(8,128)S(1)} custom-call(f32[64,64]{1,0:T(8,128)S(1)} %convolution_subtract_fusion.5), custom_call_target="Cholesky" | custom-call | tf_op jit(solution)/shard_map/jit(cholesky)/cholesky | solution.py:31
  262.8 4.0 %while.1 = (s32[]{:T(128)}, f32[320,320]{1,0:T(8,128)S(1)}, s32[2,2]{1,0:T(2,128)S(1)}, f32[2,128,128]{2,1,0:T(8,128)S(1)}, s32[]{:T(128)}) while((s32[]{:T(128)}, f32[320,320]{1,0:T(8,128)S(1)}, s32[2,2]{1,0:T(2,128)S(1)}, f32[2,128,128]{2,1,0:T(8,128)S(1)}, s32[]{:T(128)}) %tuple.29), condition=%wide.while_cond, body=%wide.while_body.sunk | while | flops 2 | bytes 131181 | solution.py:32
  263.4 1.4 bitcast_dynamic-update-slice_fusion.2
  265.3 1.4 bitcast_dynamic-update-slice_fusion.2
  268.3 29.5 %custom-call.26 = f32[3,128,128]{1,2,0:T(8,128)S(1)} custom-call(f32[3,128,128]{2,1,0:T(8,128)S(1)} %pad_maximum_fusion), custom_call_target="InvertDiagBlocksLowerTriangular" | custom-call | tf_op jit(solution)/shard_map/triangular_solve | solution.py:32
  297.8 1.4 fusion.13
  299.2 1.2 convolution_subtract_fusion.2
  300.7 1.1 convolution_subtract_fusion.4
  302.8 2.3 fusion.4
  307.2 1.4 convolution_subtract_fusion.1
  309.2 1.7 fusion
  (45 shorter events, 12.6 us)
Async XLA Ops:
  7.2 1.7 copy-start
  7.2 195.3 %all-reduce.6.cloned.1.call-start = ((), (), s32[]{:S(2)}) async-start(), calls=%async_computation | async-start | bytes 11468800 | tf_op jit(solution)/shard_map/psum | solution.py:16
  8.9 11.0 %copy-start.6 = (bf16[2048,4096]{1,0:T(8,128)(2,1)S(1)}, bf16[2048,4096]{1,0:T(8,128)(2,1)}, u32[]{:S(2)}) copy-start(bf16[2048,4096]{1,0:T(8,128)(2,1)} %param.2) | copy-start | bytes 50331652
  19.9 12.6 %copy-start.1 = (f32[2048,320]{0,1:T(8,128)}, f32[2048,320]{0,1:T(8,128)S(1)}, u32[]{:S(2)}) copy-start(f32[2048,320]{0,1:T(8,128)S(1)} %fusion.35) | copy-start | bytes 7864324
  204.8 0.8 copy-start.4
  258.3 3.3 %copy-start.3 = (f32[320,320]{1,0:T(8,128)}, f32[320,320]{1,0:T(8,128)S(1)}, u32[]{:S(2)}) copy-start(f32[320,320]{1,0:T(8,128)S(1)} %get-tuple-element.28) | copy-start | bytes 1228804
  266.7 0.7 copy-start.5
  297.8 7.3 %copy-start.2 = (f32[2048,320]{0,1:T(8,128)S(1)}, f32[2048,320]{0,1:T(8,128)}, u32[]{:S(2)}) copy-start(f32[2048,320]{0,1:T(8,128)} %copy-done.1) | copy-start | bytes 7864324
Sparse Core Ops, SparseCore 0:
  41.9 160.5 all-reduce.5
where the time goes:
time: 318 us
  waiting for transfers between devices  161 us (51%)
  other arithmetic  85.7 us (27%)
  matrix products  46.8 us (15%)
  between operations  16.2 us (5%)
  local copies, waits for them, and re-layouts  8.34 us (3%)
    psum x1, waiting for transfers between devices, total_gram(): return lax.psum(local_gram, ('grp', 'dev'))  161 us
    another operation x10, other arithmetic, local(): lower = jnp.linalg.cholesky(gram)  50.6 us
    another operation x7, other arithmetic, local(): lax.linalg.triangular_solve(lower, sketch.T, left_side=True, lower=True)  31.6 us
    dot_general x2, matrix products, contract_rows(): lax.dot_general(left, right, (((0,), (0,)), ((), ())), preferred_element_...  16.7 us
    dot_general x1, matrix products, local(): sketch = jnp.dot(slab, sketch_map, preferred_element_type=jnp.float32)  11 us
    another operation x5, matrix products, local(): lax.linalg.triangular_solve(lower, sketch.T, left_side=True, lower=True)  6.37 us
  transfers between devices with their start and end apart: 1, of which 1 were waited for; matrix products, arithmetic and copies ran while one was open for 0% of the time, Pallas kernels for 0%

commit v1 on v0

v1 whole, which is shorter than its diff:
```python
import math

import jax
import jax.numpy as jnp
from jax import lax
from jax.experimental import pallas as pl
from jax.experimental.pallas import tpu as pltpu
from jax.sharding import PartitionSpec as P

F32 = jnp.float32
BF16 = jnp.bfloat16
NN = (((1,), (0,)), ((), ()))
NT = (((1,), (1,)), ((), ()))
TN = (((0,), (0,)), ((), ()))
MESH = pl.DeviceIdType.MESH

N = 4096
SK = 320
HALF = SK // 2
LOCAL = 2048
CHUNK = 512
WIDTH = 256
SLICES = 16
SIDE = 4
TILES = 96
PIECE = TILES // 32


def dot(a, b, dims):
    return lax.dot_general(a, b, dims, preferred_element_type=F32)


def split(a):
    high = a.astype(BF16)
    return high, (a - high.astype(F32)).astype(BF16)


def dot3(a, b, dims):
    ah, al = split(a)
    bh, bl = split(b)
    return dot(ah, bh, dims) + (dot(ah, bl, dims) + dot(al, bh, dims))


def factor_block(a, n, w):
    eye = lax.broadcasted_iota(jnp.int32, (n, n), 0) == lax.broadcasted_iota(jnp.int32, (n, n), 1)
    m = jnp.concatenate([a, eye.astype(F32)], axis=1)
    width = 2 * n
    row_in_group = lax.broadcasted_iota(jnp.int32, (8, width), 0)
    per = w // 8
    groups = [m[8 * g : 8 * g + 8] for g in range(n // 8)]
    done = []
    for p in range(n // w):
        rows = groups[p * per : (p + 1) * per]
        cols = [
            [jnp.broadcast_to(r[:, p * w + l : p * w + l + 1], (8, width)) for r in rows]
            for l in range(w)
        ]
        pivots = [jnp.ones((8, width), F32) for _ in rows]
        for k in range(w):
            g, i = divmod(k, 8)
            pivot = jnp.broadcast_to(cols[k][g][i : i + 1], (8, width))
            inverse = 1.0 / pivot
            factor = {}
            for h in range(g, per):
                factor[h] = cols[k][h] * inverse
            factor[g] = jnp.where(row_in_group > i, factor[g], 0.0)
            for l in range(k + 1, w):
                value = jnp.broadcast_to(cols[l][g][i : i + 1], (8, width))
                for h in range(g, per):
                    cols[l][h] = cols[l][h] - factor[h] * value
            value = jnp.broadcast_to(rows[g][i : i + 1], (8, width))
            for h in range(g, per):
                rows[h] = rows[h] - factor[h] * value
            pivots[g] = jnp.where(row_in_group == i, pivot, pivots[g])
        block = jnp.concatenate([r * lax.rsqrt(v) for r, v in zip(rows, pivots)], axis=0)
        done.append(block[:, n:])
        if p < n // w - 1:
            high, low = split(block)
            left = jnp.concatenate([high, low, high], axis=0)[:, :n]
            right = jnp.concatenate([high, high, low], axis=0)
            update = dot(left, right, TN)
            for g in range((p + 1) * per, n // 8):
                groups[g] = groups[g] - update[8 * g : 8 * g + 8]
    return jnp.concatenate(done, axis=0)


def invert_factor(m, n, b, w):
    for k in range(n // b):
        lo, hi = k * b, (k + 1) * b
        t = factor_block(m[lo:hi, lo:hi], b, w)
        r = dot3(t, m[lo:hi, :], NN)
        parts = [r[:, :lo]] if lo else []
        parts.append(t)
        if hi < n:
            parts.append(r[:, hi:])
        r = jnp.concatenate(parts, axis=1)
        if hi < n:
            col = lax.broadcasted_iota(jnp.int32, (n - hi, n), 1)
            keep = jnp.where((col >= lo) & (col < hi), 0.0, m[hi:, :])
            m[hi:, :] = keep - dot3(r[:, hi:], r, TN)
            col = lax.broadcasted_iota(jnp.int32, (b, n), 1)
            r = jnp.where(col < hi, r, 0.0)
        m[lo:hi, :] = r


def reduce_kernel(
    slab, sketch_map,
    sketch_t, gram_out, cross_out,
    slab_v, map_v, map_t, skf, skh, gacc, gpack, gsib, gpart, gred, gline, gtot,
    cross, from_core, from_a, from_b, line,
    load_sem, map_sem, out_sem,
    g0s, g0r, g1s, g1r, g2s, g2r, g3s, g3r,
    cas, car, cbs, cbr, ccs, ccr, cds, cdr, ces, cer,
):
    g = lax.axis_index("grp")
    d = lax.axis_index("dev")
    y, c = g // 2, g % 2
    z, x = d // SIDE, d % SIDE
    other = g + 1 - 2 * c
    ma = z + c * (x - z)
    mb = x + c * (z - x)
    sa = SIDE - c * (SIDE - 1)
    sb = 1 + c * (SIDE - 1)
    lane_c = pl.multiple_of(c * HALF, 8)
    lane_o = pl.multiple_of((1 - c) * HALF, 8)

    map_copy = pltpu.make_async_copy(sketch_map, map_v, map_sem)
    map_copy.start()

    def load(i):
        rows = pl.ds(pl.multiple_of(i * CHUNK, CHUNK), CHUNK)
        return pltpu.make_async_copy(slab.at[rows, :], slab_v.at[rows, :], load_sem.at[i])

    for i in range(LOCAL // CHUNK):
        load(i).start()

    barrier = pltpu.get_barrier_semaphore()

    def greet(i, carry):
        to = lax.rem(d + i, SLICES)
        pl.semaphore_signal(barrier, inc=1, device_id=(g, to), device_id_type=MESH)
        pl.semaphore_signal(barrier, inc=1, device_id=(other, to), device_id_type=MESH)
        return carry

    lax.fori_loop(1, SLICES, greet, 0)
    pl.semaphore_signal(barrier, inc=1, device_id=(other, d), device_id_type=MESH)
    for i in range(1, SIDE):
        to = lax.rem(y + i, SIDE) * 2 + c
        pl.semaphore_signal(barrier, inc=1, device_id=(to, d), device_id_type=MESH)

    map_copy.wait()
    for i in range(N // CHUNK):
        map_t[:, i * CHUNK : (i + 1) * CHUNK] = map_v[i * CHUNK : (i + 1) * CHUNK, :].T
    gacc[...] = jnp.zeros_like(gacc)

    def sketch_chunk(i, carry):
        load(i).wait()
        rows = pl.ds(pl.multiple_of(i * CHUNK, CHUNK), CHUNK)
        s = dot(map_t[...], slab_v[rows, :], NT)
        skf[:, rows] = s
        high, low = split(s)
        skh[:, rows] = high
        gacc[...] += dot(high, high, NT) + (dot(high, low, NT) + dot(low, high, NT))
        return carry

    lax.fori_loop(0, LOCAL // CHUNK, sketch_chunk, 0)
    sketch_out = pltpu.make_async_copy(skf, sketch_t, out_sem)
    sketch_out.start()

    zero = jnp.zeros((16, 8, 128), F32)
    gpack[0:16] = gacc[0:128, 0:128].reshape(16, 8, 128)
    gpack[16:32] = gacc[0:128, 128:256].reshape(16, 8, 128)
    gpack[32:48] = zero
    gpack[32:48, :, 0:64] = gacc[0:128, 256:320].reshape(16, 8, 64)
    gpack[48:64] = gacc[128:256, 128:256].reshape(16, 8, 128)
    gpack[64:80] = zero
    gpack[64:80, :, 0:64] = gacc[128:256, 256:320].reshape(16, 8, 64)
    gpack[80:96] = zero
    gpack[80:88, :, 0:64] = gacc[256:320, 256:320].reshape(8, 8, 64)

    pl.semaphore_wait(barrier, 2 * (SLICES - 1) + 1 + SIDE - 1)

    def remote(src, dst, send, recv, to_g, to_d):
        return pltpu.make_async_remote_copy(
            src_ref=src, dst_ref=dst, send_sem=send, recv_sem=recv,
            device_id=(to_g, to_d), device_id_type=MESH,
        )

    def place(core, s):
        return jnp.where(core == 0, s, (s % SIDE) * SIDE + s // SIDE)

    def core_copy(s):
        return remote(
            cross.at[place(c, s), pl.ds(lane_o, HALF), :], from_core.at[place(1 - c, s)],
            cas.at[s], car.at[s], other, d,
        )

    def cross_block(t, carry):
        both = dot(skh[...], slab_v[:, pl.ds(pl.multiple_of(t * 2 * WIDTH, 2 * WIDTH), 2 * WIDTH)], NN)
        cross[place(c, 2 * t)] = both[:, :WIDTH]
        cross[place(c, 2 * t + 1)] = both[:, WIDTH:]
        core_copy(2 * t).start()
        core_copy(2 * t + 1).start()
        return carry

    def run_cross(first, last):
        lax.fori_loop(first, last, cross_block, 0)

    g0 = remote(gpack, gsib, g0s, g0r, other, d)
    g0.start()
    run_cross(0, 2)
    g0.wait()
    gpart[...] = gpack[...] + gsib[...]

    def g1(i):
        to = lax.rem(d + i, SLICES)
        first = c * (TILES // 2) + to * PIECE
        return remote(gpart.at[pl.ds(first, PIECE)], gred.at[i], g1s.at[i], g1r.at[i], g, to)

    def start(copy):
        def body(i, carry):
            copy(i).start()
            return carry
        return body

    def wait(copy):
        def body(i, carry):
            copy(i).wait()
            return carry
        return body

    lax.fori_loop(1, SLICES, start(g1), 0)
    run_cross(2, 5)
    lax.fori_loop(1, SLICES, wait(g1), 0)
    mine = c * (TILES // 2) + d * PIECE
    total = gpart[pl.ds(mine, PIECE)]
    for i in range(1, SLICES):
        total = total + gred[i]
    gline[pl.ds(y, 1)] = total[None]

    def g2(i):
        to = lax.rem(y + i, SIDE) * 2 + c
        return remote(gline.at[y], gline.at[y], g2s.at[i], g2r.at[i], to, d)

    lax.fori_loop(1, SIDE, start(g2), 0)
    run_cross(5, 6)
    lax.fori_loop(1, SIDE, wait(g2), 0)
    gtot[pl.ds(mine, PIECE)] = (gline[0] + gline[1]) + (gline[2] + gline[3])

    def g3(i):
        k, to = i // SLICES, lax.rem(d + i, SLICES)
        return remote(
            gtot.at[pl.ds(mine, PIECE)], gtot.at[pl.ds(mine, PIECE)],
            g3s.at[i], g3r.at[i], g + k * (other - g), to,
        )

    lax.fori_loop(1, 2 * SLICES, start(g3), 0)
    run_cross(6, 8)

    lax.fori_loop(0, SLICES, wait(core_copy), 0)

    def add_core(p):
        cross[p, pl.ds(lane_c, HALF), :] += from_core[p]

    def ca(i):
        to = lax.rem(ma + i, SIDE)
        return remote(
            cross.at[pl.ds(to * SIDE, SIDE), pl.ds(lane_c, HALF), :], from_a.at[i],
            cas.at[SLICES + i], car.at[SLICES + i], g, to * sa + mb * sb,
        )

    def ca_start(i, carry):
        to = lax.rem(ma + i, SIDE)
        for j in range(SIDE):
            add_core(to * SIDE + j)
        ca(i).start()
        return carry

    lax.fori_loop(1, SIDE, ca_start, 0)
    for j in range(SIDE):
        add_core(ma * SIDE + j)

    lax.fori_loop(1, 2 * SLICES, wait(g3), 0)
    gram_out[...] = jnp.zeros_like(gram_out)
    gram_out[0:128, 0:128] = gtot[0:16].reshape(128, 128)
    gram_out[0:128, 128:256] = gtot[16:32].reshape(128, 128)
    gram_out[0:128, 256:320] = gtot[32:48, :, 0:64].reshape(128, 64)
    gram_out[128:256, 128:256] = gtot[48:64].reshape(128, 128)
    gram_out[128:256, 256:320] = gtot[64:80, :, 0:64].reshape(128, 64)
    gram_out[256:320, 256:320] = gtot[80:88, :, 0:64].reshape(64, 64)

    lax.fori_loop(1, SIDE, wait(ca), 0)

    def add_a(j):
        p = ma * SIDE + j
        cross[p, pl.ds(lane_c, HALF), :] += (from_a[1, j] + from_a[2, j]) + from_a[3, j]

    def cb(i):
        to = lax.rem(mb + i, SIDE)
        return remote(
            cross.at[ma * SIDE + to, pl.ds(lane_c, HALF), :], from_b.at[i],
            cbs.at[i], cbr.at[i], g, ma * sa + to * sb,
        )

    def cb_start(i, carry):
        add_a(lax.rem(mb + i, SIDE))
        cb(i).start()
        return carry

    lax.fori_loop(1, SIDE, cb_start, 0)
    add_a(mb)
    lax.fori_loop(1, SIDE, wait(cb), 0)
    line[pl.ds(y, 1)] = (
        (cross[ma * SIDE + mb, pl.ds(lane_c, HALF), :] + from_b[1]) + (from_b[2] + from_b[3])
    )[None]

    def cc(i):
        to = lax.rem(y + i, SIDE) * 2 + c
        return remote(line.at[y], line.at[y], ccs.at[i], ccr.at[i], to, d)

    lax.fori_loop(1, SIDE, start(cc), 0)
    lax.fori_loop(1, SIDE, wait(cc), 0)
    cross_out[pl.ds(lane_c, HALF), :] = (line[0] + line[1]) + (line[2] + line[3])

    rows = pl.ds(lane_c, HALF)
    last = remote(cross_out.at[rows, :], cross_out.at[rows, :], ces, cer, other, d)
    last.start()
    last.wait()
    sketch_out.wait()


def reduce_call(slab, sketch_map):
    dma = pltpu.SemaphoreType.DMA
    return pl.pallas_call(
        reduce_kernel,
        out_shape=(
            jax.ShapeDtypeStruct((SK, LOCAL), F32),
            jax.ShapeDtypeStruct((SK, SK), F32),
            jax.ShapeDtypeStruct((SK, WIDTH), F32),
        ),
        in_specs=[pl.BlockSpec(memory_space=pl.ANY)] * 2,
        out_specs=(
            pl.BlockSpec(memory_space=pl.ANY),
            pl.BlockSpec(memory_space=pltpu.VMEM),
            pl.BlockSpec(memory_space=pltpu.VMEM),
        ),
        scratch_shapes=[
            pltpu.VMEM((LOCAL, N), BF16),
            pltpu.VMEM((N, SK), BF16),
            pltpu.VMEM((SK, N), BF16),
            pltpu.VMEM((SK, LOCAL), F32),
            pltpu.VMEM((SK, LOCAL), BF16),
            pltpu.VMEM((SK, SK), F32),
            pltpu.VMEM((TILES, 8, 128), F32),
            pltpu.VMEM((TILES, 8, 128), F32),
            pltpu.VMEM((TILES, 8, 128), F32),
            pltpu.VMEM((SLICES, PIECE, 8, 128), F32),
            pltpu.VMEM((SIDE, PIECE, 8, 128), F32),
            pltpu.VMEM((TILES, 8, 128), F32),
            pltpu.VMEM((SLICES, SK, WIDTH), F32),
            pltpu.VMEM((SLICES, HALF, WIDTH), F32),
            pltpu.VMEM((SIDE, SIDE, HALF, WIDTH), F32),
            pltpu.VMEM((SIDE, HALF, WIDTH), F32),
            pltpu.VMEM((SIDE, HALF, WIDTH), F32),
            dma((LOCAL // CHUNK,)), dma, dma,
            dma, dma,
            dma((SLICES,)), dma((SLICES,)),
            dma((SIDE,)), dma((SIDE,)),
            dma((2 * SLICES,)), dma((2 * SLICES,)),
            dma((SLICES + SIDE,)), dma((SLICES + SIDE,)),
            dma((SIDE,)), dma((SIDE,)),
            dma((SIDE,)), dma((SIDE,)),
            dma((SIDE,)), dma((SIDE,)),
            dma, dma,
        ],
        compiler_params=pltpu.CompilerParams(
            collective_id=0, has_side_effects=True, vmem_limit_bytes=58 << 20
        ),
        cost_estimate=pl.CostEstimate(
            flops=4 * LOCAL * N * SK, bytes_accessed=24 << 20, transcendentals=0
        ),
        name="sketch_and_sums",
    )(slab, sketch_map)


def finish_kernel(scale, gram, cross, sketch_t, basis, coeffs, m, skf, out, load_sem, out_sem):
    load = pltpu.make_async_copy(sketch_t, skf, load_sem)
    load.start()
    m[...] = gram[...]
    invert_factor(m, SK, 64, 16)
    coeffs[...] = dot3(m[...], cross[...], NN) * (1.0 / scale)
    high, low = split(m[...] * scale)
    load.wait()

    def store(i):
        rows = pl.ds(i * CHUNK, CHUNK)
        return pltpu.make_async_copy(out.at[rows, :], basis.at[rows, :], out_sem.at[i])

    for i in range(LOCAL // CHUNK):
        sh, sl = split(skf[:, i * CHUNK : (i + 1) * CHUNK])
        b = dot(high, sh, NN) + (dot(high, sl, NN) + dot(low, sh, NN))
        out[i * CHUNK : (i + 1) * CHUNK, :] = b.T
        store(i).start()
    for i in range(LOCAL // CHUNK):
        store(i).wait()


def finish_call(scale, gram, cross, sketch_t):
    def kernel(*refs):
        finish_kernel(scale, *refs)

    vmem = pl.BlockSpec(memory_space=pltpu.VMEM)
    hbm = pl.BlockSpec(memory_space=pl.ANY)
    return pl.pallas_call(
        kernel,
        out_shape=(
            jax.ShapeDtypeStruct((LOCAL, SK), F32),
            jax.ShapeDtypeStruct((SK, WIDTH), F32),
        ),
        in_specs=[vmem, vmem, hbm],
        out_specs=(hbm, vmem),
        scratch_shapes=[
            pltpu.VMEM((SK, SK), F32),
            pltpu.VMEM((SK, LOCAL), F32),
            pltpu.VMEM((LOCAL, SK), F32),
            pltpu.SemaphoreType.DMA,
            pltpu.SemaphoreType.DMA((LOCAL // CHUNK,)),
        ],
        compiler_params=pltpu.CompilerParams(vmem_limit_bytes=48 << 20),
        name="factor_and_basis",
    )(gram, cross, sketch_t)


def local(slab, sketch_map):
    rows = slab.shape[0] * lax.axis_size("grp") * lax.axis_size("dev")
    scale = math.sqrt(rows)
    sketch_t, gram, cross = reduce_call(slab, sketch_map)
    return finish_call(scale, gram, cross, sketch_t)


def solution(mesh):
    in_specs = (P(("grp", "dev"), None), P())
    out_specs = (P(("grp", "dev"), None), P(None, "dev"))
    return jax.shard_map(local, mesh=mesh, in_specs=in_specs, out_specs=out_specs, check_vma=False)
```

time: 318 us -> 99.7 us (0.31)
  waiting for transfers between devices: 161 us -> 0 us
  Pallas kernels: 0 us -> 87 us
  other arithmetic: 85.7 us -> 0 us
  matrix products: 46.8 us -> 0 us
  between operations: 16.2 us -> 0.66 us
  local copies, waits for them, and re-layouts: 8.34 us -> 11.7 us
    psum x1 -> x0, waiting for transfers between devices: 161 us -> none  [total_gram(): return lax.psum(local_gram, ('grp', 'dev'))]
    pallas_call x0 -> x2, Pallas kernels: none -> 87 us  [the longest x1 71.2 us: reduce_call(): pl.pallas_call(reduce_kernel, out_shape=(jax.ShapeDtypeStruct((SK, LOCAL)...]
    another operation x17 -> x0, other arithmetic: 82.1 us -> none  [the longest x10 50.6 us: local(): lower = jnp.linalg.cholesky(gram)]
    dot_general x4 -> x0, matrix products: 32.8 us -> none  [the longest x2 16.7 us: contract_rows(): lax.dot_general(left, right, (((0,), (0,)), ((), ())), preferred_element_...]
    another operation x14 -> x0, matrix products: 14 us -> none  [the longest x5 6.37 us: local(): lax.linalg.triangular_solve(lower, sketch.T, left_side=True, lower=True)]
    unnamed x14 -> x7, local copies, waits for them, and re-layouts: 3.05 us -> 8.28 us
    another operation x11 -> x0, local copies, waits for them, and re-layouts: 4.05 us -> none
    pallas_call x0 -> x1, local copies, waits for them, and re-layouts: none -> 3.4 us  [finish_call(): pl.pallas_call(kernel, out_shape=(jax.ShapeDtypeStruct((LOCAL, SK), F32),...]
  transfers between devices with their start and end apart: 1 -> 0, of which waited for: 1 -> 0; matrix products, arithmetic and copies ran while one was open for 0% -> 0% of each run, Pallas kernels for 0% -> 0%
where the time goes in v1:
time: 99.7 us; the launch traced here: 99.4 us
  Pallas kernels  87 us (87%)
  local copies, waits for them, and re-layouts  11.7 us (12%)
    pallas_call x1, Pallas kernels, reduce_call(): pl.pallas_call(reduce_kernel, out_shape=(jax.ShapeDtypeStruct((SK, LOCAL)...  71.2 us
    pallas_call x1, Pallas kernels, finish_call(): pl.pallas_call(kernel, out_shape=(jax.ShapeDtypeStruct((LOCAL, SK), F32),...  15.8 us
    unnamed x7, local copies, waits for them, and re-layouts  8.28 us
    pallas_call x1, local copies, waits for them, and re-layouts, finish_call(): pl.pallas_call(kernel, out_shape=(jax.ShapeDtypeStruct((LOCAL, SK), F32),...  3.4 us

profile of v1, /device:TPU:1, one launch (start us, length us, event | category | flops | bytes accessed | tf_op | source)
XLA Modules:
  0.0 99.4 jit_solution(15791488554109571677)
XLA Ops:
  0.6 4.5 %copy.4.sketch_map = bf16[4096,320]{1,0:T(8,128)(2,1)} copy(bf16[4096,320]{0,1:T(8,128)(2,1)} %param.3) | data formatting | bytes 5242880 | tf_op args[1]
  5.2 71.2 %sketch_and_sums.1 = (f32[320,2048]{1,0:T(8,128)}, f32[320,320]{1,0:T(8,128)}, f32[320,256]{1,0:T(8,128)}) custom-call(bf16[2048,4096]{1,0:T(8,128)(2,1)} %slab.1, bf16[4096,320]{1,0:T(8,128)(2,1)} %copy.4.sketch_map), custom_call_target="tpu_custom_call" | custom-call | flops 10737418240 | bytes 25165824 | tf_op jit(solution)/shard_map/sketch_and_sums/pallas_call | solution.py:334
  76.4 0.0 copy-start
  76.4 1.7 %copy-done = f32[320,2048]{1,0:T(8,128)S(1)} copy-done((f32[320,2048]{1,0:T(8,128)S(1)}, f32[320,2048]{1,0:T(8,128)}, u32[]{:S(2)}) %copy-start) | copy-done | bytes 2621464
  78.1 0.0 copy-start.1
  78.2 1.0 %copy-done.1 = f32[320,320]{1,0:T(8,128)S(1)} copy-done((f32[320,320]{1,0:T(8,128)S(1)}, f32[320,320]{1,0:T(8,128)}, u32[]{:S(2)}) %copy-start.1) | copy-done | bytes 409624
  79.2 0.0 copy-start.2
  79.2 1.0 copy-done.2
  80.2 15.8 %factor_and_basis.1 = (f32[2048,320]{1,0:T(8,128)}, f32[320,256]{1,0:T(8,128)}) custom-call(f32[320,320]{1,0:T(8,128)S(1)} %copy-done.1, f32[320,256]{1,0:T(8,128)S(1)} %copy-done.2, f32[320,2048]{1,0:T(8,128)S(1)} %copy-done), custom_call_target="tpu_custom_call" | custom-call | tf_op jit(solution)/shard_map/factor_and_basis/pallas_call | solution.py:414
  96.0 3.4 %copy.5 = f32[2048,320]{0,1:T(8,128)} copy(f32[2048,320]{1,0:T(8,128)} %get-tuple-element.8) | data formatting | bytes 5242880 | tf_op jit(solution)/shard_map/factor_and_basis/pallas_call | solution.py:414
Async XLA Ops:
  76.4 1.7 %copy-start = (f32[320,2048]{1,0:T(8,128)S(1)}, f32[320,2048]{1,0:T(8,128)}, u32[]{:S(2)}) copy-start(f32[320,2048]{1,0:T(8,128)} %get-tuple-element.7.refs_2_) | copy-start | bytes 7864324
  78.1 1.0 %copy-start.1 = (f32[320,320]{1,0:T(8,128)S(1)}, f32[320,320]{1,0:T(8,128)}, u32[]{:S(2)}) copy-start(f32[320,320]{1,0:T(8,128)} %get-tuple-element.5.refs_0_) | copy-start | bytes 1228804
  79.2 1.0 copy-start.2

commit v2 on v1

v2 whole, which is shorter than its diff:
```python
import math

import jax
import jax.numpy as jnp
from jax import lax
from jax.experimental import pallas as pl
from jax.experimental.pallas import tpu as pltpu
from jax.sharding import PartitionSpec as P

F32 = jnp.float32
BF16 = jnp.bfloat16
NN = (((1,), (0,)), ((), ()))
NT = (((1,), (1,)), ((), ()))
TN = (((0,), (0,)), ((), ()))
MESH = pl.DeviceIdType.MESH

N = 4096
SK = 320
HALF = SK // 2
LOCAL = 2048
CHUNK = 512
WIDTH = 256
SLICES = 16
SIDE = 4


def dot(a, b, dims):
    return lax.dot_general(a, b, dims, preferred_element_type=F32)


def split(a):
    high = a.astype(BF16)
    return high, (a - high.astype(F32)).astype(BF16)


def dot3(a, b, dims):
    ah, al = split(a)
    bh, bl = split(b)
    return dot(ah, bh, dims) + (dot(ah, bl, dims) + dot(al, bh, dims))


def factor_block(a, n, w):
    eye = lax.broadcasted_iota(jnp.int32, (n, n), 0) == lax.broadcasted_iota(jnp.int32, (n, n), 1)
    m = jnp.concatenate([a, eye.astype(F32)], axis=1)
    width = 2 * n
    row_in_group = lax.broadcasted_iota(jnp.int32, (8, width), 0)
    per = w // 8
    groups = [m[8 * g : 8 * g + 8] for g in range(n // 8)]
    done = []
    for p in range(n // w):
        rows = groups[p * per : (p + 1) * per]
        cols = [
            [jnp.broadcast_to(r[:, p * w + l : p * w + l + 1], (8, width)) for r in rows]
            for l in range(w)
        ]
        pivots = [jnp.ones((8, width), F32) for _ in rows]
        for k in range(w):
            g, i = divmod(k, 8)
            pivot = jnp.broadcast_to(cols[k][g][i : i + 1], (8, width))
            inverse = 1.0 / pivot
            factor = {}
            for h in range(g, per):
                factor[h] = cols[k][h] * inverse
            factor[g] = jnp.where(row_in_group > i, factor[g], 0.0)
            for l in range(k + 1, w):
                value = jnp.broadcast_to(cols[l][g][i : i + 1], (8, width))
                for h in range(g, per):
                    cols[l][h] = cols[l][h] - factor[h] * value
            value = jnp.broadcast_to(rows[g][i : i + 1], (8, width))
            for h in range(g, per):
                rows[h] = rows[h] - factor[h] * value
            pivots[g] = jnp.where(row_in_group == i, pivot, pivots[g])
        block = jnp.concatenate([r * lax.rsqrt(v) for r, v in zip(rows, pivots)], axis=0)
        done.append(block[:, n:])
        if p < n // w - 1:
            high, low = split(block)
            left = jnp.concatenate([high, low, high], axis=0)[:, :n]
            right = jnp.concatenate([high, high, low], axis=0)
            update = dot(left, right, TN)
            for g in range((p + 1) * per, n // 8):
                groups[g] = groups[g] - update[8 * g : 8 * g + 8]
    return jnp.concatenate(done, axis=0)


def invert_step(m, k, n, b, w):
    lo, hi = k * b, (k + 1) * b
    t = factor_block(m[lo:hi, lo:hi], b, w)
    r = dot3(t, m[lo:hi, :], NN)
    parts = [r[:, :lo]] if lo else []
    parts.append(t)
    if hi < n:
        parts.append(r[:, hi:])
    r = jnp.concatenate(parts, axis=1)
    if hi < n:
        col = lax.broadcasted_iota(jnp.int32, (n - hi, n), 1)
        keep = jnp.where((col >= lo) & (col < hi), 0.0, m[hi:, :])
        m[hi:, :] = keep - dot3(r[:, hi:], r, TN)
        col = lax.broadcasted_iota(jnp.int32, (b, n), 1)
        r = jnp.where(col < hi, r, 0.0)
    m[lo:hi, :] = r


DIST = (0, 1, 2, 1)
AROUND = sorted(
    ((i, j) for i in range(SIDE) for j in range(SIDE) if (i, j) != (0, 0)),
    key=lambda p: -(DIST[p[0]] + DIST[p[1]]),
)
CELLS = (
    [(2, j) for j in range(4)] + [(0, 2), (1, 2), (3, 2)]
    + [(1, 0), (1, 1), (1, 3), (0, 1), (3, 1)]
    + [(3, 0), (3, 3), (0, 3)]
    + [(0, 0)]
)
BLOCK = 64
EVEN = [(i, j) for j in (0, 2, 4) for i in range(j + 1)]
ODD = [(i, j) for j in (1, 3) for i in range(j + 1)]
PACK = [(i, j, n, 0) for n, (i, j) in enumerate(EVEN[:8])]
PACK += [(i, j, n, 1) for n, (i, j) in enumerate(ODD + EVEN[8:])]
TILES = 64
PIECE = TILES // 32
PART = HALF // SIDE


def table(q, values):
    return sum(jnp.where(q == k, v, 0) for k, v in enumerate(values) if v)


def reduce_kernel(
    slab, map_rows,
    sketch_t, m, cross_out,
    slab_v, map_t, skf, skh, skl, gpack, gsib, gred, gline, gtot,
    cross, from_core, from_a, from_b, line, from_y,
    load_sem, map_sem, out_sem,
    g0s, g0r, g1s, g1r, g2s, g2r, g3s, g3r, g4s, g4r,
    xs, xr, as_, ar, bs, br, ys, yr, zs, zr,
):
    g = lax.axis_index("grp")
    d = lax.axis_index("dev")
    y, c = g // 2, g % 2
    z, x = d // SIDE, d % SIDE
    other = g + 1 - 2 * c
    row_c = pl.multiple_of(c * HALF, 8)
    row_o = pl.multiple_of((1 - c) * HALF, 8)
    mine = pl.ds(row_c, HALF)

    map_copy = pltpu.make_async_copy(map_rows, map_t, map_sem)
    map_copy.start()

    def load(i):
        rows = pl.ds(pl.multiple_of(i * CHUNK, CHUNK), CHUNK)
        return pltpu.make_async_copy(slab.at[rows, :], slab_v.at[rows, :], load_sem.at[i])

    load(0).start()
    load(1).start()

    def chip(dz, dx):
        return lax.rem(z + dz, SIDE) * SIDE + lax.rem(x + dx, SIDE)

    def along_a(i):
        return jnp.where(c == 0, chip(i, 0), chip(0, i))

    def along_b(i):
        return jnp.where(c == 0, chip(0, i), chip(i, 0))

    def along_y(i, core):
        return lax.rem(y + i, SIDE) * 2 + core

    barrier = pltpu.get_barrier_semaphore()

    def greet(to_g, to_d):
        pl.semaphore_signal(barrier, inc=1, device_id=(to_g, to_d), device_id_type=MESH)

    for dz, dx in AROUND:
        greet(g, chip(dz, dx))
    for i in range(1, SIDE):
        greet(along_y(i, c), d)
    for i in range(SIDE):
        greet(along_y(i, 1 - c), d)

    map_copy.wait()

    def sketch_chunk(i, carry):
        load(i).wait()

        @pl.when(i + 2 < LOCAL // CHUNK)
        def _():
            load(i + 2).start()

        rows = pl.ds(pl.multiple_of(i * CHUNK, CHUNK), CHUNK)
        s = dot(map_t[...], slab_v[rows, :], NT)
        skf[:, rows] = s
        high, low = split(s)
        skh[:, rows] = high
        skl[:, rows] = low
        return carry

    lax.fori_loop(0, LOCAL // CHUNK, sketch_chunk, 0)
    sketch_out = pltpu.make_async_copy(skf, sketch_t, out_sem)
    sketch_out.start()

    mixed = dot(skl[...], skh[...], NT)
    gram = dot(skh[...], skh[...], NT) + (mixed + mixed.T)
    gpack[56:64] = jnp.zeros((8, 8, 128), F32)
    for i, j, n, h in PACK:
        block = gram[i * BLOCK : (i + 1) * BLOCK, j * BLOCK : (j + 1) * BLOCK]
        gpack[8 * n : 8 * n + 8, :, h * BLOCK : (h + 1) * BLOCK] = block.reshape(8, 8, BLOCK)

    pl.semaphore_wait(barrier, len(AROUND) + 2 * SIDE - 1)

    def remote(src, dst, send, recv, to_g, to_d):
        return pltpu.make_async_remote_copy(
            src_ref=src, dst_ref=dst, send_sem=send, recv_sem=recv,
            device_id=(to_g, to_d), device_id_type=MESH,
        )

    def core_copy(q):
        dz, dx = table(q, [p[0] for p in CELLS]), table(q, [p[1] for p in CELLS])
        here = jnp.where(c == 0, dz * SIDE + dx, dx * SIDE + dz)
        there = jnp.where(c == 0, dx * SIDE + dz, dz * SIDE + dx)
        return remote(
            cross.at[here, pl.ds(row_o, HALF), :], from_core.at[there],
            xs.at[q], xr.at[q], other, d,
        )

    def cross_cell(q, carry):
        dz, dx = table(q, [p[0] for p in CELLS]), table(q, [p[1] for p in CELLS])
        here = jnp.where(c == 0, dz * SIDE + dx, dx * SIDE + dz)
        columns = pl.ds(pl.multiple_of(chip(dz, dx) * WIDTH, WIDTH), WIDTH)
        cross[here] = dot(skh[...], slab_v[:, columns], NN)
        core_copy(q).start()
        return carry

    def run_cross(first, last):
        lax.fori_loop(first, last, cross_cell, 0)

    def cross_arrived(first, last):
        def body(q, carry):
            core_copy(q).wait()
            return carry
        lax.fori_loop(first, last, body, 0)

    def add_core(p):
        cross[p, mine, :] += from_core[p]

    g0 = remote(gpack, gsib, g0s, g0r, other, d)
    g0.start()
    run_cross(0, 3)
    g0.wait()
    gsib[...] = gpack[...] + gsib[...]

    def g1(dz, dx):
        to = chip(dz, dx)
        k = dz * SIDE + dx
        part = pl.ds(c * (TILES // 2) + to * PIECE, PIECE)
        return remote(gsib.at[part], gred.at[k], g1s.at[k], g1r.at[k], g, to)

    for p in AROUND:
        g1(*p).start()
    run_cross(3, 8)

    def a_copy(k):
        first = (8, 10, 6, 12, 4, 14)[k]
        to = along_a(1 if k % 2 == 0 else SIDE - 1)
        return remote(
            cross.at[pl.ds(first, 2), mine, :], from_a.at[k], as_.at[k], ar.at[k], g, to
        )

    cross_arrived(0, 7)
    for p in range(8, 12):
        add_core(p)
    a_copy(0).start()
    a_copy(1).start()
    run_cross(8, 16)

    for p in AROUND[::-1]:
        g1(*p).wait()
    part = pl.ds(c * (TILES // 2) + d * PIECE, PIECE)
    total = gsib[part]
    for dz, dx in AROUND:
        total = total + gred[dz * SIDE + dx]
    gline[pl.ds(y, 1)] = total[None]

    def g2(i):
        return remote(gline.at[y], gline.at[y], g2s.at[i], g2r.at[i], along_y(i, c), d)

    for i in (2, 1, 3):
        g2(i).start()

    cross_arrived(7, 16)
    for p in (4, 5, 6, 7, 12, 13, 14, 15):
        add_core(p)
    a_copy(2).start()
    a_copy(3).start()
    for p in range(4):
        add_core(p)

    for i in (1, 3, 2):
        g2(i).wait()
    gtot[part] = (gline[0] + gline[1]) + (gline[2] + gline[3])

    def g3(dz, dx):
        k = dz * SIDE + dx
        return remote(gtot.at[part], gtot.at[part], g3s.at[k], g3r.at[k], g, chip(dz, dx))

    for p in AROUND:
        g3(*p).start()

    a_copy(0).wait()
    a_copy(1).wait()
    cross[4:6, mine, :] += from_a[0]
    cross[14:16, mine, :] += from_a[1]
    a_copy(4).start()
    a_copy(5).start()

    for p in AROUND[::-1]:
        g3(*p).wait()
    half = pl.ds(c * (TILES // 2), TILES // 2)
    g4 = remote(gtot.at[half], gtot.at[half], g4s, g4r, other, d)
    g4.start()
    m[...] = jnp.zeros_like(m)
    g4.wait()
    for i, j, n, h in PACK:
        block = gtot[8 * n : 8 * n + 8, :, h * BLOCK : (h + 1) * BLOCK].reshape(BLOCK, BLOCK)
        m[i * BLOCK : (i + 1) * BLOCK, j * BLOCK : (j + 1) * BLOCK] = block

    def factor_step(k):
        invert_step(m, k, SK, BLOCK, 16)

    factor_step(0)

    for k in range(2, 6):
        a_copy(k).wait()
    cross[0:2, mine, :] += from_a[4] + from_a[3]
    cross[2:4, mine, :] += from_a[2] + from_a[5]

    def b_copy(i):
        return remote(cross.at[i, mine, :], from_b.at[i], bs.at[i], br.at[i], g, along_b(i))

    for i in (2, 1, 3):
        b_copy(i).start()
    factor_step(1)
    for i in (1, 3, 2):
        b_copy(i).wait()
    line[...] = (cross[0, mine, :] + from_b[1]) + (from_b[2] + from_b[3])

    def y_copy(i):
        rows = pl.ds(pl.multiple_of(lax.rem(y + i, SIDE) * PART, 8), PART)
        return remote(line.at[rows, :], from_y.at[i], ys.at[i], yr.at[i], along_y(i, c), d)

    for i in (2, 1, 3):
        y_copy(i).start()
    factor_step(2)
    for i in (1, 3, 2):
        y_copy(i).wait()
    own = line[pl.ds(pl.multiple_of(y * PART, 8), PART), :]
    final = pl.ds(pl.multiple_of(c * HALF + y * PART, 8), PART)
    cross_out[final, :] = (own + from_y[1]) + (from_y[2] + from_y[3])

    def z_copy(k):
        i, flip = k % SIDE, k // SIDE
        core = c + flip * (1 - 2 * c)
        return remote(
            cross_out.at[final, :], cross_out.at[final, :], zs.at[k], zr.at[k],
            along_y(i, core), d,
        )

    for k in range(1, 2 * SIDE):
        z_copy(k).start()
    factor_step(3)
    factor_step(4)
    for k in range(1, 2 * SIDE):
        z_copy(k).wait()
    sketch_out.wait()


def reduce_call(slab, map_rows):
    dma = pltpu.SemaphoreType.DMA
    return pl.pallas_call(
        reduce_kernel,
        out_shape=(
            jax.ShapeDtypeStruct((SK, LOCAL), F32),
            jax.ShapeDtypeStruct((SK, SK), F32),
            jax.ShapeDtypeStruct((SK, WIDTH), F32),
        ),
        in_specs=[pl.BlockSpec(memory_space=pl.ANY)] * 2,
        out_specs=(
            pl.BlockSpec(memory_space=pl.ANY),
            pl.BlockSpec(memory_space=pltpu.VMEM),
            pl.BlockSpec(memory_space=pltpu.VMEM),
        ),
        scratch_shapes=[
            pltpu.VMEM((LOCAL, N), BF16),
            pltpu.VMEM((SK, N), BF16),
            pltpu.VMEM((SK, LOCAL), F32),
            pltpu.VMEM((SK, LOCAL), BF16),
            pltpu.VMEM((SK, LOCAL), BF16),
            pltpu.VMEM((TILES, 8, 128), F32),
            pltpu.VMEM((TILES, 8, 128), F32),
            pltpu.VMEM((SLICES, PIECE, 8, 128), F32),
            pltpu.VMEM((SIDE, PIECE, 8, 128), F32),
            pltpu.VMEM((TILES, 8, 128), F32),
            pltpu.VMEM((SLICES, SK, WIDTH), F32),
            pltpu.VMEM((SLICES, HALF, WIDTH), F32),
            pltpu.VMEM((6, 2, HALF, WIDTH), F32),
            pltpu.VMEM((SIDE, HALF, WIDTH), F32),
            pltpu.VMEM((HALF, WIDTH), F32),
            pltpu.VMEM((SIDE, PART, WIDTH), F32),
            dma((LOCAL // CHUNK,)), dma, dma,
            dma, dma,
            dma((SLICES,)), dma((SLICES,)),
            dma((SIDE,)), dma((SIDE,)),
            dma((SLICES,)), dma((SLICES,)),
            dma, dma,
            dma((SLICES,)), dma((SLICES,)),
            dma((6,)), dma((6,)),
            dma((SIDE,)), dma((SIDE,)),
            dma((SIDE,)), dma((SIDE,)),
            dma((2 * SIDE,)), dma((2 * SIDE,)),
        ],
        compiler_params=pltpu.CompilerParams(
            collective_id=0, has_side_effects=True, vmem_limit_bytes=58 << 20
        ),
        cost_estimate=pl.CostEstimate(
            flops=4 * LOCAL * N * SK, bytes_accessed=24 << 20, transcendentals=0
        ),
        name="sketch_and_sums",
    )(slab, map_rows)


def finish_kernel(scale, inverse, cross, sketch_t, basis_t, coeffs, m, cr, skf, out, m_sem, cross_sem, load_sem, out_sem):
    m_copy = pltpu.make_async_copy(inverse, m, m_sem)
    m_copy.start()
    cross_copy = pltpu.make_async_copy(cross, cr, cross_sem)
    cross_copy.start()
    load = pltpu.make_async_copy(sketch_t, skf, load_sem)
    load.start()
    m_copy.wait()
    high, low = split(m[...] * scale)
    load.wait()

    def store(i):
        part = pl.ds(i * CHUNK, CHUNK)
        return pltpu.make_async_copy(out.at[:, part], basis_t.at[:, part], out_sem.at[i])

    for i in range(LOCAL // CHUNK):
        part = slice(i * CHUNK, (i + 1) * CHUNK)
        sh, sl = split(skf[:, part])
        out[:, part] = dot(high, sh, NN) + (dot(high, sl, NN) + dot(low, sh, NN))
        store(i).start()
    cross_copy.wait()
    coeffs[...] = dot3(m[...], cr[...], NN) * (1.0 / scale)
    for i in range(LOCAL // CHUNK):
        store(i).wait()


def finish_call(scale, inverse, cross, sketch_t):
    def kernel(*refs):
        finish_kernel(scale, *refs)

    vmem = pl.BlockSpec(memory_space=pltpu.VMEM)
    hbm = pl.BlockSpec(memory_space=pl.ANY)
    dma = pltpu.SemaphoreType.DMA
    return pl.pallas_call(
        kernel,
        out_shape=(
            jax.ShapeDtypeStruct((SK, LOCAL), F32),
            jax.ShapeDtypeStruct((SK, WIDTH), F32),
        ),
        in_specs=[hbm, hbm, hbm],
        out_specs=(hbm, vmem),
        scratch_shapes=[
            pltpu.VMEM((SK, SK), F32),
            pltpu.VMEM((SK, WIDTH), F32),
            pltpu.VMEM((SK, LOCAL), F32),
            pltpu.VMEM((SK, LOCAL), F32),
            dma, dma, dma,
            dma((LOCAL // CHUNK,)),
        ],
        compiler_params=pltpu.CompilerParams(vmem_limit_bytes=60 << 20),
        name="basis_and_coeffs",
    )(inverse, cross, sketch_t)


def local(slab, sketch_map):
    rows = slab.shape[0] * lax.axis_size("grp") * lax.axis_size("dev")
    scale = math.sqrt(rows)
    sketch_t, inverse, cross = reduce_call(slab, sketch_map.T)
    basis_t, coeffs = finish_call(scale, inverse, cross, sketch_t)
    return basis_t.T, coeffs


def solution(mesh):
    in_specs = (P(("grp", "dev"), None), P())
    out_specs = (P(("grp", "dev"), None), P(None, "dev"))
    return jax.shard_map(local, mesh=mesh, in_specs=in_specs, out_specs=out_specs, check_vma=False)
```

time: 99.7 us -> 64.3 us (0.64)
  Pallas kernels: 87 us -> 63.5 us
  local copies, waits for them, and re-layouts: 11.7 us -> 0 us
    pallas_call x1, Pallas kernels: 71.2 us -> 57.4 us  [reduce_call(): pl.pallas_call(reduce_kernel, out_shape=(jax.ShapeDtypeStruct((SK, LOCAL)...]
    pallas_call x1, Pallas kernels: 15.8 us -> 6.1 us  [finish_call(): pl.pallas_call(kernel, out_shape=(jax.ShapeDtypeStruct((SK, LOCAL), F32),...]
    unnamed x7 -> x0, local copies, waits for them, and re-layouts: 8.28 us -> none
    pallas_call x1 -> x0, local copies, waits for them, and re-layouts: 3.4 us -> none  [finish_call(): pl.pallas_call(kernel, out_shape=(jax.ShapeDtypeStruct((LOCAL, SK), F32),...]
where the time goes in v2:
time: 64.3 us; the launch traced here: 64.2 us
  Pallas kernels  63.5 us (99%)
    pallas_call x1, Pallas kernels, reduce_call(): pl.pallas_call(reduce_kernel, out_shape=(jax.ShapeDtypeStruct((SK, LOCAL)...  57.4 us
    pallas_call x1, Pallas kernels, finish_call(): pl.pallas_call(kernel, out_shape=(jax.ShapeDtypeStruct((SK, LOCAL), F32),...  6.1 us

profile of v2, /device:TPU:1, one launch (start us, length us, event | category | flops | bytes accessed | tf_op | source)
XLA Modules:
  0.0 64.2 jit_solution(14585431862453143225)
XLA Ops:
  0.6 57.4 %sketch_and_sums.1 = (f32[320,2048]{1,0:T(8,128)}, f32[320,320]{1,0:T(8,128)}, f32[320,256]{1,0:T(8,128)}) custom-call(bf16[2048,4096]{1,0:T(8,128)(2,1)} %slab.1, bf16[320,4096]{1,0:T(8,128)(2,1)} %bitcast.2), custom_call_target="tpu_custom_call" | custom-call | flops 10737418240 | bytes 25165824 | tf_op jit(solution)/shard_map/sketch_and_sums/pallas_call | solution.py:378
  58.1 6.1 %basis_and_coeffs.1 = (f32[320,2048]{1,0:T(8,128)}, f32[320,256]{1,0:T(8,128)}) custom-call(f32[320,320]{1,0:T(8,128)} %get-tuple-element.7.refs_0_, f32[320,256]{1,0:T(8,128)} %get-tuple-element.8.refs_1_, f32[320,2048]{1,0:T(8,128)} %get-tuple-element.9.refs_2_), custom_call_target="tpu_custom_call" | custom-call | tf_op jit(solution)/shard_map/basis_and_coeffs/pallas_call | solution.py:463

commit v3 on v2

--- a/solution.py
+++ b/solution.py
@@ -128,7 +128,7 @@
 def reduce_kernel(
     slab, map_rows,
     sketch_t, m, cross_out,
-    slab_v, map_t, skf, skh, skl, gpack, gsib, gred, gline, gtot,
+    slab_v, map_t, parts, gpack, gsib, gred, gline, gtot,
     cross, from_core, from_a, from_b, line, from_y,
     load_sem, map_sem, out_sem,
     g0s, g0r, g1s, g1r, g2s, g2r, g3s, g3r, g4s, g4r,
@@ -188,18 +188,17 @@
 
         rows = pl.ds(pl.multiple_of(i * CHUNK, CHUNK), CHUNK)
         s = dot(map_t[...], slab_v[rows, :], NT)
-        skf[:, rows] = s
         high, low = split(s)
-        skh[:, rows] = high
-        skl[:, rows] = low
+        parts[:SK, rows] = high
+        parts[SK:, rows] = low
         return carry
 
     lax.fori_loop(0, LOCAL // CHUNK, sketch_chunk, 0)
-    sketch_out = pltpu.make_async_copy(skf, sketch_t, out_sem)
+    sketch_out = pltpu.make_async_copy(parts, sketch_t, out_sem)
     sketch_out.start()
 
-    mixed = dot(skl[...], skh[...], NT)
-    gram = dot(skh[...], skh[...], NT) + (mixed + mixed.T)
+    mixed = dot(parts[SK:], parts[:SK], NT)
+    gram = dot(parts[:SK], parts[:SK], NT) + (mixed + mixed.T)
     gpack[56:64] = jnp.zeros((8, 8, 128), F32)
     for i, j, n, h in PACK:
         block = gram[i * BLOCK : (i + 1) * BLOCK, j * BLOCK : (j + 1) * BLOCK]
@@ -226,7 +225,7 @@
         dz, dx = table(q, [p[0] for p in CELLS]), table(q, [p[1] for p in CELLS])
         here = jnp.where(c == 0, dz * SIDE + dx, dx * SIDE + dz)
         columns = pl.ds(pl.multiple_of(chip(dz, dx) * WIDTH, WIDTH), WIDTH)
-        cross[here] = dot(skh[...], slab_v[:, columns], NN)
+        cross[here] = dot(parts[:SK], slab_v[:, columns], NN)
         core_copy(q).start()
         return carry
 
@@ -256,7 +255,7 @@
 
     for p in AROUND:
         g1(*p).start()
-    run_cross(3, 8)
+    run_cross(3, 7)
 
     def a_copy(k):
         first = (8, 10, 6, 12, 4, 14)[k]
@@ -270,7 +269,16 @@
         add_core(p)
     a_copy(0).start()
     a_copy(1).start()
-    run_cross(8, 16)
+    run_cross(7, 12)
+    cross_arrived(7, 12)
+    for p in range(4, 8):
+        add_core(p)
+    a_copy(2).start()
+    run_cross(12, 16)
+    cross_arrived(12, 15)
+    for p in range(12, 16):
+        add_core(p)
+    a_copy(3).start()
 
     for p in AROUND[::-1]:
         g1(*p).wait()
@@ -286,31 +294,37 @@
     for i in (2, 1, 3):
         g2(i).start()
 
-    cross_arrived(7, 16)
-    for p in (4, 5, 6, 7, 12, 13, 14, 15):
-        add_core(p)
-    a_copy(2).start()
-    a_copy(3).start()
-    for p in range(4):
-        add_core(p)
-
-    for i in (1, 3, 2):
-        g2(i).wait()
-    gtot[part] = (gline[0] + gline[1]) + (gline[2] + gline[3])
-
-    def g3(dz, dx):
-        k = dz * SIDE + dx
-        return remote(gtot.at[part], gtot.at[part], g3s.at[k], g3r.at[k], g, chip(dz, dx))
-
-    for p in AROUND:
-        g3(*p).start()
-
     a_copy(0).wait()
     a_copy(1).wait()
     cross[4:6, mine, :] += from_a[0]
     cross[14:16, mine, :] += from_a[1]
     a_copy(4).start()
     a_copy(5).start()
+    cross_arrived(15, 16)
+    for p in range(4):
+        add_core(p)
+
+    for i in (1, 3, 2):
+        g2(i).wait()
+    gtot[part] = (gline[0] + gline[1]) + (gline[2] + gline[3])
+
+    def g3(dz, dx):
+        k = dz * SIDE + dx
+        return remote(gtot.at[part], gtot.at[part], g3s.at[k], g3r.at[k], g, chip(dz, dx))
+
+    for p in AROUND:
+        g3(*p).start()
+
+    for k in range(2, 6):
+        a_copy(k).wait()
+    cross[0:2, mine, :] += from_a[4] + from_a[3]
+    cross[2:4, mine, :] += from_a[2] + from_a[5]
+
+    def b_copy(i):
+        return remote(cross.at[i, mine, :], from_b.at[i], bs.at[i], br.at[i], g, along_b(i))
+
+    for i in (2, 1, 3):
+        b_copy(i).start()
 
     for p in AROUND[::-1]:
         g3(*p).wait()
@@ -326,19 +340,6 @@
     def factor_step(k):
         invert_step(m, k, SK, BLOCK, 16)
 
-    factor_step(0)
-
-    for k in range(2, 6):
-        a_copy(k).wait()
-    cross[0:2, mine, :] += from_a[4] + from_a[3]
-    cross[2:4, mine, :] += from_a[2] + from_a[5]
-
-    def b_copy(i):
-        return remote(cross.at[i, mine, :], from_b.at[i], bs.at[i], br.at[i], g, along_b(i))
-
-    for i in (2, 1, 3):
-        b_copy(i).start()
-    factor_step(1)
     for i in (1, 3, 2):
         b_copy(i).wait()
     line[...] = (cross[0, mine, :] + from_b[1]) + (from_b[2] + from_b[3])
@@ -349,7 +350,8 @@
 
     for i in (2, 1, 3):
         y_copy(i).start()
-    factor_step(2)
+    factor_step(0)
+    factor_step(1)
     for i in (1, 3, 2):
         y_copy(i).wait()
     own = line[pl.ds(pl.multiple_of(y * PART, 8), PART), :]
@@ -366,6 +368,7 @@
 
     for k in range(1, 2 * SIDE):
         z_copy(k).start()
+    factor_step(2)
     factor_step(3)
     factor_step(4)
     for k in range(1, 2 * SIDE):
@@ -378,7 +381,7 @@
     return pl.pallas_call(
         reduce_kernel,
         out_shape=(
-            jax.ShapeDtypeStruct((SK, LOCAL), F32),
+            jax.ShapeDtypeStruct((2 * SK, LOCAL), BF16),
             jax.ShapeDtypeStruct((SK, SK), F32),
             jax.ShapeDtypeStruct((SK, WIDTH), F32),
         ),
@@ -391,9 +394,7 @@
         scratch_shapes=[
             pltpu.VMEM((LOCAL, N), BF16),
             pltpu.VMEM((SK, N), BF16),
-            pltpu.VMEM((SK, LOCAL), F32),
-            pltpu.VMEM((SK, LOCAL), BF16),
-            pltpu.VMEM((SK, LOCAL), BF16),
+            pltpu.VMEM((2 * SK, LOCAL), BF16),
             pltpu.VMEM((TILES, 8, 128), F32),
             pltpu.VMEM((TILES, 8, 128), F32),
             pltpu.VMEM((SLICES, PIECE, 8, 128), F32),
@@ -427,25 +428,33 @@
     )(slab, map_rows)
 
 
-def finish_kernel(scale, inverse, cross, sketch_t, basis_t, coeffs, m, cr, skf, out, m_sem, cross_sem, load_sem, out_sem):
+def finish_kernel(
+    scale, inverse, cross, sketch_t, basis_t, coeffs, m, cr, parts, out, m_sem, cross_sem, load_sem, out_sem
+):
     m_copy = pltpu.make_async_copy(inverse, m, m_sem)
     m_copy.start()
+
+    def load(i):
+        part = pl.ds(pl.multiple_of(i * CHUNK, CHUNK), CHUNK)
+        return pltpu.make_async_copy(sketch_t.at[:, part], parts.at[:, part], load_sem.at[i])
+
+    for i in range(LOCAL // CHUNK):
+        load(i).start()
     cross_copy = pltpu.make_async_copy(cross, cr, cross_sem)
     cross_copy.start()
-    load = pltpu.make_async_copy(sketch_t, skf, load_sem)
-    load.start()
     m_copy.wait()
     high, low = split(m[...] * scale)
-    load.wait()
+    left = jnp.concatenate([high, high, low], axis=1)
 
     def store(i):
+        part = pl.ds(pl.multiple_of(i * CHUNK, CHUNK), CHUNK)
+        return pltpu.make_async_copy(out.at[:, part], basis_t.at[:, part], out_sem.at[i])
+
+    for i in range(LOCAL // CHUNK):
         part = pl.ds(i * CHUNK, CHUNK)
-        return pltpu.make_async_copy(out.at[:, part], basis_t.at[:, part], out_sem.at[i])
-
-    for i in range(LOCAL // CHUNK):
-        part = slice(i * CHUNK, (i + 1) * CHUNK)
-        sh, sl = split(skf[:, part])
-        out[:, part] = dot(high, sh, NN) + (dot(high, sl, NN) + dot(low, sh, NN))
+        load(i).wait()
+        right = jnp.concatenate([parts[:, part], parts[:SK, part]], axis=0)
+        out[:, part] = dot(left, right, NN)
         store(i).start()
     cross_copy.wait()
     coeffs[...] = dot3(m[...], cr[...], NN) * (1.0 / scale)
@@ -471,10 +480,10 @@
         scratch_shapes=[
             pltpu.VMEM((SK, SK), F32),
             pltpu.VMEM((SK, WIDTH), F32),
+            pltpu.VMEM((2 * SK, LOCAL), BF16),
             pltpu.VMEM((SK, LOCAL), F32),
-            pltpu.VMEM((SK, LOCAL), F32),
-            dma, dma, dma,
-            dma((LOCAL // CHUNK,)),
+            dma, dma,
+            dma((LOCAL // CHUNK,)), dma((LOCAL // CHUNK,)),
         ],
         compiler_params=pltpu.CompilerParams(vmem_limit_bytes=60 << 20),
         name="basis_and_coeffs",

time: 64.3 us -> 64 us (level)
  no operation moved by 1% of the time
where the time goes in v3:
time: 64 us; the launch traced here: 63.9 us
  Pallas kernels  63.1 us (99%)
  between operations  0.8 us (1%)
    pallas_call x1, Pallas kernels, reduce_call(): pl.pallas_call(reduce_kernel, out_shape=(jax.ShapeDtypeStruct((2 * SK, LO...  57.4 us
    pallas_call x1, Pallas kernels, finish_call(): pl.pallas_call(kernel, out_shape=(jax.ShapeDtypeStruct((SK, LOCAL), F32),...  5.7 us

profile of v3, /device:TPU:1, one launch (start us, length us, event | category | flops | bytes accessed | tf_op | source)
XLA Modules:
  0.0 63.9 jit_solution(8859195564341600161)
XLA Ops:
  0.6 57.4 %sketch_and_sums.1 = (bf16[640,2048]{1,0:T(8,128)(2,1)}, f32[320,320]{1,0:T(8,128)}, f32[320,256]{1,0:T(8,128)}) custom-call(bf16[2048,4096]{1,0:T(8,128)(2,1)} %slab.1, bf16[320,4096]{1,0:T(8,128)(2,1)} %bitcast.2), custom_call_target="tpu_custom_call" | custom-call | flops 10737418240 | bytes 25165824 | tf_op jit(solution)/shard_map/sketch_and_sums/pallas_call | solution.py:381
  58.0 5.7 %basis_and_coeffs.1 = (f32[320,2048]{1,0:T(8,128)}, f32[320,256]{1,0:T(8,128)}) custom-call(f32[320,320]{1,0:T(8,128)} %get-tuple-element.7.refs_0_, f32[320,256]{1,0:T(8,128)} %get-tuple-element.8.refs_1_, bf16[640,2048]{1,0:T(8,128)(2,1)} %get-tuple-element.9.refs_2_), custom_call_target="tpu_custom_call" | custom-call | tf_op jit(solution)/shard_map/basis_and_coeffs/pallas_call | solution.py:472

commit v4 on v3

--- a/solution.py
+++ b/solution.py
@@ -47,38 +47,35 @@
     per = w // 8
     groups = [m[8 * g : 8 * g + 8] for g in range(n // 8)]
     done = []
+
+    def spread(value, i):
+        return jnp.broadcast_to(value[i : i + 1], (8, width))
+
     for p in range(n // w):
-        rows = groups[p * per : (p + 1) * per]
+        rows = groups[p * per :]
         cols = [
             [jnp.broadcast_to(r[:, p * w + l : p * w + l + 1], (8, width)) for r in rows]
             for l in range(w)
         ]
-        pivots = [jnp.ones((8, width), F32) for _ in rows]
+        pivots = [jnp.ones((8, width), F32) for _ in range(per)]
         for k in range(w):
             g, i = divmod(k, 8)
-            pivot = jnp.broadcast_to(cols[k][g][i : i + 1], (8, width))
+            pivot = spread(cols[k][g], i)
             inverse = 1.0 / pivot
-            factor = {}
-            for h in range(g, per):
-                factor[h] = cols[k][h] * inverse
+            left = range(g, len(rows))
+            factor = {h: cols[k][h] * inverse for h in left}
             factor[g] = jnp.where(row_in_group > i, factor[g], 0.0)
             for l in range(k + 1, w):
-                value = jnp.broadcast_to(cols[l][g][i : i + 1], (8, width))
-                for h in range(g, per):
+                value = spread(cols[l][g], i)
+                for h in left:
                     cols[l][h] = cols[l][h] - factor[h] * value
-            value = jnp.broadcast_to(rows[g][i : i + 1], (8, width))
-            for h in range(g, per):
+            value = spread(rows[g], i)
+            for h in left:
                 rows[h] = rows[h] - factor[h] * value
             pivots[g] = jnp.where(row_in_group == i, pivot, pivots[g])
-        block = jnp.concatenate([r * lax.rsqrt(v) for r, v in zip(rows, pivots)], axis=0)
-        done.append(block[:, n:])
-        if p < n // w - 1:
-            high, low = split(block)
-            left = jnp.concatenate([high, low, high], axis=0)[:, :n]
-            right = jnp.concatenate([high, high, low], axis=0)
-            update = dot(left, right, TN)
-            for g in range((p + 1) * per, n // 8):
-                groups[g] = groups[g] - update[8 * g : 8 * g + 8]
+        for h in range(per):
+            done.append((rows[h] * lax.rsqrt(pivots[h]))[:, n:])
+        groups[p * per :] = rows
     return jnp.concatenate(done, axis=0)
 
 
@@ -131,7 +128,7 @@
     slab_v, map_t, parts, gpack, gsib, gred, gline, gtot,
     cross, from_core, from_a, from_b, line, from_y,
     load_sem, map_sem, out_sem,
-    g0s, g0r, g1s, g1r, g2s, g2r, g3s, g3r, g4s, g4r,
+    g0s, g0r, g1s, g1r, g2s, g2r, g3s, g3r,
     xs, xr, as_, ar, bs, br, ys, yr, zs, zr,
 ):
     g = lax.axis_index("grp")
@@ -172,6 +169,7 @@
 
     for dz, dx in AROUND:
         greet(g, chip(dz, dx))
+        greet(other, chip(dz, dx))
     for i in range(1, SIDE):
         greet(along_y(i, c), d)
     for i in range(SIDE):
@@ -204,7 +202,7 @@
         block = gram[i * BLOCK : (i + 1) * BLOCK, j * BLOCK : (j + 1) * BLOCK]
         gpack[8 * n : 8 * n + 8, :, h * BLOCK : (h + 1) * BLOCK] = block.reshape(8, 8, BLOCK)
 
-    pl.semaphore_wait(barrier, len(AROUND) + 2 * SIDE - 1)
+    pl.semaphore_wait(barrier, 2 * len(AROUND) + 2 * SIDE - 1)
 
     def remote(src, dst, send, recv, to_g, to_d):
         return pltpu.make_async_remote_copy(
@@ -221,16 +219,23 @@
             xs.at[q], xr.at[q], other, d,
         )
 
-    def cross_cell(q, carry):
+    def cross_cell(q):
         dz, dx = table(q, [p[0] for p in CELLS]), table(q, [p[1] for p in CELLS])
         here = jnp.where(c == 0, dz * SIDE + dx, dx * SIDE + dz)
         columns = pl.ds(pl.multiple_of(chip(dz, dx) * WIDTH, WIDTH), WIDTH)
-        cross[here] = dot(parts[:SK], slab_v[:, columns], NN)
-        core_copy(q).start()
+        return here, dot(parts[:SK], slab_v[:, columns], NN)
+
+    def cross_pair(t, carry):
+        first, a = cross_cell(2 * t)
+        second, b = cross_cell(2 * t + 1)
+        cross[first] = a
+        cross[second] = b
+        core_copy(2 * t).start()
+        core_copy(2 * t + 1).start()
         return carry
 
     def run_cross(first, last):
-        lax.fori_loop(first, last, cross_cell, 0)
+        lax.fori_loop(first // 2, last // 2, cross_pair, 0)
 
     def cross_arrived(first, last):
         def body(q, carry):
@@ -243,7 +248,7 @@
 
     g0 = remote(gpack, gsib, g0s, g0r, other, d)
     g0.start()
-    run_cross(0, 3)
+    run_cross(0, 4)
     g0.wait()
     gsib[...] = gpack[...] + gsib[...]
 
@@ -255,7 +260,7 @@
 
     for p in AROUND:
         g1(*p).start()
-    run_cross(3, 7)
+    run_cross(4, 8)
 
     def a_copy(k):
         first = (8, 10, 6, 12, 4, 14)[k]
@@ -269,7 +274,7 @@
         add_core(p)
     a_copy(0).start()
     a_copy(1).start()
-    run_cross(7, 12)
+    run_cross(8, 12)
     cross_arrived(7, 12)
     for p in range(4, 8):
         add_core(p)
@@ -308,11 +313,13 @@
         g2(i).wait()
     gtot[part] = (gline[0] + gline[1]) + (gline[2] + gline[3])
 
-    def g3(dz, dx):
-        k = dz * SIDE + dx
-        return remote(gtot.at[part], gtot.at[part], g3s.at[k], g3r.at[k], g, chip(dz, dx))
-
-    for p in AROUND:
+    def g3(flip, dz, dx):
+        k = flip * SLICES + dz * SIDE + dx
+        to_g = other if flip else g
+        return remote(gtot.at[part], gtot.at[part], g3s.at[k], g3r.at[k], to_g, chip(dz, dx))
+
+    handed = [(flip, dz, dx) for dz, dx in AROUND for flip in (0, 1)] + [(1, 0, 0)]
+    for p in handed:
         g3(*p).start()
 
     for k in range(2, 6):
@@ -326,13 +333,9 @@
     for i in (2, 1, 3):
         b_copy(i).start()
 
-    for p in AROUND[::-1]:
+    m[...] = jnp.zeros_like(m)
+    for p in handed[::-1]:
         g3(*p).wait()
-    half = pl.ds(c * (TILES // 2), TILES // 2)
-    g4 = remote(gtot.at[half], gtot.at[half], g4s, g4r, other, d)
-    g4.start()
-    m[...] = jnp.zeros_like(m)
-    g4.wait()
     for i, j, n, h in PACK:
         block = gtot[8 * n : 8 * n + 8, :, h * BLOCK : (h + 1) * BLOCK].reshape(BLOCK, BLOCK)
         m[i * BLOCK : (i + 1) * BLOCK, j * BLOCK : (j + 1) * BLOCK] = block
@@ -410,8 +413,7 @@
             dma, dma,
             dma((SLICES,)), dma((SLICES,)),
             dma((SIDE,)), dma((SIDE,)),
-            dma((SLICES,)), dma((SLICES,)),
-            dma, dma,
+            dma((2 * SLICES,)), dma((2 * SLICES,)),
             dma((SLICES,)), dma((SLICES,)),
             dma((6,)), dma((6,)),
             dma((SIDE,)), dma((SIDE,)),

time: 64 us -> 63.8 us (level)
  no operation moved by 1% of the time
where the time goes in v4:
time: 63.8 us; the launch traced here: 63.7 us
  Pallas kernels  62.9 us (99%)
  between operations  0.8 us (1%)
    pallas_call x1, Pallas kernels, reduce_call(): pl.pallas_call(reduce_kernel, out_shape=(jax.ShapeDtypeStruct((2 * SK, LO...  57.2 us
    pallas_call x1, Pallas kernels, finish_call(): pl.pallas_call(kernel, out_shape=(jax.ShapeDtypeStruct((SK, LOCAL), F32),...  5.7 us

profile of v4, /device:TPU:1, one launch (start us, length us, event | category | flops | bytes accessed | tf_op | source)
XLA Modules:
  0.0 63.7 jit_solution(7889365324423819693)
XLA Ops:
  0.6 57.2 %sketch_and_sums.1 = (bf16[640,2048]{1,0:T(8,128)(2,1)}, f32[320,320]{1,0:T(8,128)}, f32[320,256]{1,0:T(8,128)}) custom-call(bf16[2048,4096]{1,0:T(8,128)(2,1)} %slab.1, bf16[320,4096]{1,0:T(8,128)(2,1)} %bitcast.2), custom_call_target="tpu_custom_call" | custom-call | flops 10737418240 | bytes 25165824 | tf_op jit(solution)/shard_map/sketch_and_sums/pallas_call | solution.py:384
  57.8 5.7 %basis_and_coeffs.1 = (f32[320,2048]{1,0:T(8,128)}, f32[320,256]{1,0:T(8,128)}) custom-call(f32[320,320]{1,0:T(8,128)} %get-tuple-element.7.refs_0_, f32[320,256]{1,0:T(8,128)} %get-tuple-element.8.refs_1_, bf16[640,2048]{1,0:T(8,128)(2,1)} %get-tuple-element.9.refs_2_), custom_call_target="tpu_custom_call" | custom-call | tf_op jit(solution)/shard_map/basis_and_coeffs/pallas_call | solution.py:474

commit v5 on v4

--- a/solution.py
+++ b/solution.py
@@ -19,6 +19,7 @@
 HALF = SK // 2
 LOCAL = 2048
 CHUNK = 512
+STEP = 1024
 WIDTH = 256
 SLICES = 16
 SIDE = 4
@@ -280,10 +281,6 @@
         add_core(p)
     a_copy(2).start()
     run_cross(12, 16)
-    cross_arrived(12, 15)
-    for p in range(12, 16):
-        add_core(p)
-    a_copy(3).start()
 
     for p in AROUND[::-1]:
         g1(*p).wait()
@@ -299,28 +296,33 @@
     for i in (2, 1, 3):
         g2(i).start()
 
+    cross_arrived(12, 16)
+    for p in range(12, 16):
+        add_core(p)
+    a_copy(3).start()
+    for p in range(4):
+        add_core(p)
+
+    for i in (1, 3, 2):
+        g2(i).wait()
+    gtot[part] = (gline[0] + gline[1]) + (gline[2] + gline[3])
+
+    def g3(flip, dz, dx):
+        k = flip * SLICES + dz * SIDE + dx
+        to_g = other if flip else g
+        return remote(gtot.at[part], gtot.at[part], g3s.at[k], g3r.at[k], to_g, chip(dz, dx))
+
+    handed = [(flip, dz, dx) for dz, dx in AROUND for flip in (0, 1)] + [(1, 0, 0)]
+    for p in handed:
+        g3(*p).start()
+
     a_copy(0).wait()
     a_copy(1).wait()
     cross[4:6, mine, :] += from_a[0]
     cross[14:16, mine, :] += from_a[1]
     a_copy(4).start()
     a_copy(5).start()
-    cross_arrived(15, 16)
-    for p in range(4):
-        add_core(p)
-
-    for i in (1, 3, 2):
-        g2(i).wait()
-    gtot[part] = (gline[0] + gline[1]) + (gline[2] + gline[3])
-
-    def g3(flip, dz, dx):
-        k = flip * SLICES + dz * SIDE + dx
-        to_g = other if flip else g
-        return remote(gtot.at[part], gtot.at[part], g3s.at[k], g3r.at[k], to_g, chip(dz, dx))
-
-    handed = [(flip, dz, dx) for dz, dx in AROUND for flip in (0, 1)] + [(1, 0, 0)]
-    for p in handed:
-        g3(*p).start()
+    m[...] = jnp.zeros_like(m)
 
     for k in range(2, 6):
         a_copy(k).wait()
@@ -333,7 +335,6 @@
     for i in (2, 1, 3):
         b_copy(i).start()
 
-    m[...] = jnp.zeros_like(m)
     for p in handed[::-1]:
         g3(*p).wait()
     for i, j, n, h in PACK:
@@ -343,6 +344,7 @@
     def factor_step(k):
         invert_step(m, k, SK, BLOCK, 16)
 
+    factor_step(0)
     for i in (1, 3, 2):
         b_copy(i).wait()
     line[...] = (cross[0, mine, :] + from_b[1]) + (from_b[2] + from_b[3])
@@ -353,8 +355,8 @@
 
     for i in (2, 1, 3):
         y_copy(i).start()
-    factor_step(0)
     factor_step(1)
+    factor_step(2)
     for i in (1, 3, 2):
         y_copy(i).wait()
     own = line[pl.ds(pl.multiple_of(y * PART, 8), PART), :]
@@ -371,7 +373,6 @@
 
     for k in range(1, 2 * SIDE):
         z_copy(k).start()
-    factor_step(2)
     factor_step(3)
     factor_step(4)
     for k in range(1, 2 * SIDE):
@@ -431,36 +432,39 @@
 
 
 def finish_kernel(
-    scale, inverse, cross, sketch_t, basis_t, coeffs, m, cr, parts, out, m_sem, cross_sem, load_sem, out_sem
+    scale, inverse, cross, sketch_t, basis_t, coeffs, m, cr, lefts, parts, out, m_sem, cross_sem, load_sem, out_sem
 ):
     m_copy = pltpu.make_async_copy(inverse, m, m_sem)
     m_copy.start()
 
     def load(i):
-        part = pl.ds(pl.multiple_of(i * CHUNK, CHUNK), CHUNK)
+        part = pl.ds(pl.multiple_of(i * STEP, STEP), STEP)
         return pltpu.make_async_copy(sketch_t.at[:, part], parts.at[:, part], load_sem.at[i])
 
-    for i in range(LOCAL // CHUNK):
+    for i in range(LOCAL // STEP):
         load(i).start()
     cross_copy = pltpu.make_async_copy(cross, cr, cross_sem)
     cross_copy.start()
     m_copy.wait()
     high, low = split(m[...] * scale)
-    left = jnp.concatenate([high, high, low], axis=1)
+    lefts[...] = jnp.concatenate([high, high, low], axis=1)
 
     def store(i):
-        part = pl.ds(pl.multiple_of(i * CHUNK, CHUNK), CHUNK)
+        part = pl.ds(pl.multiple_of(i * STEP, STEP), STEP)
         return pltpu.make_async_copy(out.at[:, part], basis_t.at[:, part], out_sem.at[i])
 
-    for i in range(LOCAL // CHUNK):
-        part = pl.ds(i * CHUNK, CHUNK)
+    def basis_chunk(i, carry):
+        part = pl.ds(pl.multiple_of(i * STEP, STEP), STEP)
         load(i).wait()
         right = jnp.concatenate([parts[:, part], parts[:SK, part]], axis=0)
-        out[:, part] = dot(left, right, NN)
+        out[:, part] = dot(lefts[...], right, NN)
         store(i).start()
+        return carry
+
+    lax.fori_loop(0, LOCAL // STEP, basis_chunk, 0)
     cross_copy.wait()
     coeffs[...] = dot3(m[...], cr[...], NN) * (1.0 / scale)
-    for i in range(LOCAL // CHUNK):
+    for i in range(LOCAL // STEP):
         store(i).wait()
 
 
@@ -482,10 +486,11 @@
         scratch_shapes=[
             pltpu.VMEM((SK, SK), F32),
             pltpu.VMEM((SK, WIDTH), F32),
+            pltpu.VMEM((SK, 3 * SK), BF16),
             pltpu.VMEM((2 * SK, LOCAL), BF16),
             pltpu.VMEM((SK, LOCAL), F32),
             dma, dma,
-            dma((LOCAL // CHUNK,)), dma((LOCAL // CHUNK,)),
+            dma((LOCAL // STEP,)), dma((LOCAL // STEP,)),
         ],
         compiler_params=pltpu.CompilerParams(vmem_limit_bytes=60 << 20),
         name="basis_and_coeffs",

time: 63.8 us -> 64.4 us (level)
    pallas_call x1, Pallas kernels: 57.2 us -> 58.4 us  [reduce_call(): pl.pallas_call(reduce_kernel, out_shape=(jax.ShapeDtypeStruct((2 * SK, LO...]
where the time goes in v5:
time: 64.4 us; the launch traced here: 64.3 us
  Pallas kernels  63.5 us (99%)
  between operations  0.8 us (1%)
    pallas_call x1, Pallas kernels, reduce_call(): pl.pallas_call(reduce_kernel, out_shape=(jax.ShapeDtypeStruct((2 * SK, LO...  58.4 us
    pallas_call x1, Pallas kernels, finish_call(): pl.pallas_call(kernel, out_shape=(jax.ShapeDtypeStruct((SK, LOCAL), F32),...  5.08 us

profile of v5, /device:TPU:1, one launch (start us, length us, event | category | flops | bytes accessed | tf_op | source)
XLA Modules:
  0.0 64.3 jit_solution(7147790553127349133)
XLA Ops:
  0.6 58.4 %sketch_and_sums.1 = (bf16[640,2048]{1,0:T(8,128)(2,1)}, f32[320,320]{1,0:T(8,128)}, f32[320,256]{1,0:T(8,128)}) custom-call(bf16[2048,4096]{1,0:T(8,128)(2,1)} %slab.1, bf16[320,4096]{1,0:T(8,128)(2,1)} %bitcast.2), custom_call_target="tpu_custom_call" | custom-call | flops 10737418240 | bytes 25165824 | tf_op jit(solution)/shard_map/sketch_and_sums/pallas_call | solution.py:385
  59.1 5.1 %basis_and_coeffs.1 = (f32[320,2048]{1,0:T(8,128)}, f32[320,256]{1,0:T(8,128)}) custom-call(f32[320,320]{1,0:T(8,128)} %get-tuple-element.7.refs_0_, f32[320,256]{1,0:T(8,128)} %get-tuple-element.8.refs_1_, bf16[640,2048]{1,0:T(8,128)(2,1)} %get-tuple-element.9.refs_2_), custom_call_target="tpu_custom_call" | custom-call | tf_op jit(solution)/shard_map/basis_and_coeffs/pallas_call | solution.py:478

commit v6 on v5

--- a/solution.py
+++ b/solution.py
@@ -119,14 +119,22 @@
 PART = HALF // SIDE
 
 
+def wait_store(store):
+    def body(i, carry):
+        store(i).wait()
+        return carry
+
+    return body
+
+
 def table(q, values):
     return sum(jnp.where(q == k, v, 0) for k, v in enumerate(values) if v)
 
 
-def reduce_kernel(
-    slab, map_rows,
-    sketch_t, m, cross_out,
-    slab_v, map_t, parts, gpack, gsib, gred, gline, gtot,
+def whole_kernel(
+    scale, slab, map_rows,
+    basis_t, coeffs,
+    m, cross_out, left, out, slab_v, map_t, parts, gpack, gsib, gred, gline, gtot,
     cross, from_core, from_a, from_b, line, from_y,
     load_sem, map_sem, out_sem,
     g0s, g0r, g1s, g1r, g2s, g2r, g3s, g3r,
@@ -193,8 +201,6 @@
         return carry
 
     lax.fori_loop(0, LOCAL // CHUNK, sketch_chunk, 0)
-    sketch_out = pltpu.make_async_copy(parts, sketch_t, out_sem)
-    sketch_out.start()
 
     mixed = dot(parts[SK:], parts[:SK], NT)
     gram = dot(parts[:SK], parts[:SK], NT) + (mixed + mixed.T)
@@ -375,27 +381,49 @@
         z_copy(k).start()
     factor_step(3)
     factor_step(4)
+
+    high, low = split(m[...] * scale)
+    left[...] = jnp.concatenate([high, high, low], axis=1)
+
+    def store(i):
+        part = pl.ds(pl.multiple_of(i * STEP, STEP), STEP)
+        return pltpu.make_async_copy(out.at[:, part], basis_t.at[:, part], out_sem.at[i])
+
+    def basis_step(i, carry):
+        part = pl.ds(pl.multiple_of(i * STEP, STEP), STEP)
+        right = jnp.concatenate([parts[:, part], parts[:SK, part]], axis=0)
+        out[:, part] = dot(left[...], right, NN)
+        store(i).start()
+        return carry
+
+    lax.fori_loop(0, LOCAL // STEP, basis_step, 0)
     for k in range(1, 2 * SIDE):
         z_copy(k).wait()
-    sketch_out.wait()
-
-
-def reduce_call(slab, map_rows):
+    coeffs[...] = dot3(m[...], cross_out[...], NN) * (1.0 / scale)
+    lax.fori_loop(0, LOCAL // STEP, wait_store(store), 0)
+
+
+def whole_call(scale, slab, map_rows):
+    def kernel(*refs):
+        whole_kernel(scale, *refs)
+
     dma = pltpu.SemaphoreType.DMA
     return pl.pallas_call(
-        reduce_kernel,
+        kernel,
         out_shape=(
-            jax.ShapeDtypeStruct((2 * SK, LOCAL), BF16),
-            jax.ShapeDtypeStruct((SK, SK), F32),
+            jax.ShapeDtypeStruct((SK, LOCAL), F32),
             jax.ShapeDtypeStruct((SK, WIDTH), F32),
         ),
         in_specs=[pl.BlockSpec(memory_space=pl.ANY)] * 2,
         out_specs=(
             pl.BlockSpec(memory_space=pl.ANY),
             pl.BlockSpec(memory_space=pltpu.VMEM),
-            pl.BlockSpec(memory_space=pltpu.VMEM),
         ),
         scratch_shapes=[
+            pltpu.VMEM((SK, SK), F32),
+            pltpu.VMEM((SK, WIDTH), F32),
+            pltpu.VMEM((SK, 3 * SK), BF16),
+            pltpu.VMEM((SK, LOCAL), F32),
             pltpu.VMEM((LOCAL, N), BF16),
             pltpu.VMEM((SK, N), BF16),
             pltpu.VMEM((2 * SK, LOCAL), BF16),
@@ -410,7 +438,7 @@
             pltpu.VMEM((SIDE, HALF, WIDTH), F32),
             pltpu.VMEM((HALF, WIDTH), F32),
             pltpu.VMEM((SIDE, PART, WIDTH), F32),
-            dma((LOCAL // CHUNK,)), dma, dma,
+            dma((LOCAL // CHUNK,)), dma, dma((LOCAL // STEP,)),
             dma, dma,
             dma((SLICES,)), dma((SLICES,)),
             dma((SIDE,)), dma((SIDE,)),
@@ -427,81 +455,14 @@
         cost_estimate=pl.CostEstimate(
             flops=4 * LOCAL * N * SK, bytes_accessed=24 << 20, transcendentals=0
         ),
-        name="sketch_and_sums",
+        name="range_finder",
     )(slab, map_rows)
-
-
-def finish_kernel(
-    scale, inverse, cross, sketch_t, basis_t, coeffs, m, cr, lefts, parts, out, m_sem, cross_sem, load_sem, out_sem
-):
-    m_copy = pltpu.make_async_copy(inverse, m, m_sem)
-    m_copy.start()
-
-    def load(i):
-        part = pl.ds(pl.multiple_of(i * STEP, STEP), STEP)
-        return pltpu.make_async_copy(sketch_t.at[:, part], parts.at[:, part], load_sem.at[i])
-
-    for i in range(LOCAL // STEP):
-        load(i).start()
-    cross_copy = pltpu.make_async_copy(cross, cr, cross_sem)
-    cross_copy.start()
-    m_copy.wait()
-    high, low = split(m[...] * scale)
-    lefts[...] = jnp.concatenate([high, high, low], axis=1)
-
-    def store(i):
-        part = pl.ds(pl.multiple_of(i * STEP, STEP), STEP)
-        return pltpu.make_async_copy(out.at[:, part], basis_t.at[:, part], out_sem.at[i])
-
-    def basis_chunk(i, carry):
-        part = pl.ds(pl.multiple_of(i * STEP, STEP), STEP)
-        load(i).wait()
-        right = jnp.concatenate([parts[:, part], parts[:SK, part]], axis=0)
-        out[:, part] = dot(lefts[...], right, NN)
-        store(i).start()
-        return carry
-
-    lax.fori_loop(0, LOCAL // STEP, basis_chunk, 0)
-    cross_copy.wait()
-    coeffs[...] = dot3(m[...], cr[...], NN) * (1.0 / scale)
-    for i in range(LOCAL // STEP):
-        store(i).wait()
-
-
-def finish_call(scale, inverse, cross, sketch_t):
-    def kernel(*refs):
-        finish_kernel(scale, *refs)
-
-    vmem = pl.BlockSpec(memory_space=pltpu.VMEM)
-    hbm = pl.BlockSpec(memory_space=pl.ANY)
-    dma = pltpu.SemaphoreType.DMA
-    return pl.pallas_call(
-        kernel,
-        out_shape=(
-            jax.ShapeDtypeStruct((SK, LOCAL), F32),
-            jax.ShapeDtypeStruct((SK, WIDTH), F32),
-        ),
-        in_specs=[hbm, hbm, hbm],
-        out_specs=(hbm, vmem),
-        scratch_shapes=[
-            pltpu.VMEM((SK, SK), F32),
-            pltpu.VMEM((SK, WIDTH), F32),
-            pltpu.VMEM((SK, 3 * SK), BF16),
-            pltpu.VMEM((2 * SK, LOCAL), BF16),
-            pltpu.VMEM((SK, LOCAL), F32),
-            dma, dma,
-            dma((LOCAL // STEP,)), dma((LOCAL // STEP,)),
-        ],
-        compiler_params=pltpu.CompilerParams(vmem_limit_bytes=60 << 20),
-        name="basis_and_coeffs",
-    )(inverse, cross, sketch_t)
 
 
 def local(slab, sketch_map):
     rows = slab.shape[0] * lax.axis_size("grp") * lax.axis_size("dev")
     scale = math.sqrt(rows)
-    sketch_t, inverse, cross = reduce_call(slab, sketch_map.T)
-    basis_t, coeffs = finish_call(scale, inverse, cross, sketch_t)
+    basis_t, coeffs = whole_call(scale, slab, sketch_map.T)
     return basis_t.T, coeffs
 
 

time: 64.4 us -> 63.8 us (level)
  Pallas kernels: 63.5 us -> 58.7 us
  local copies, waits for them, and re-layouts: 0 us -> 4.31 us
    pallas_call x2 -> x1, Pallas kernels: 63.5 us -> 58.7 us  [whole_call(): pl.pallas_call(kernel, out_shape=(jax.ShapeDtypeStruct((SK, LOCAL), F32),...]
    unnamed x0 -> x4, local copies, waits for them, and re-layouts: none -> 4.31 us
where the time goes in v6:
time: 63.8 us; the launch traced here: 63.6 us
  Pallas kernels  58.7 us (92%)
  local copies, waits for them, and re-layouts  4.31 us (7%)
  between operations  0.65 us (1%)
    pallas_call x1, Pallas kernels, whole_call(): pl.pallas_call(kernel, out_shape=(jax.ShapeDtypeStruct((SK, LOCAL), F32),...  58.7 us
    unnamed x4, local copies, waits for them, and re-layouts  4.31 us

profile of v6, /device:TPU:1, one launch (start us, length us, event | category | flops | bytes accessed | tf_op | source)
XLA Modules:
  0.0 63.6 jit_solution(7562344316554014012)
XLA Ops:
  0.6 58.7 %range_finder.1 = (f32[320,2048]{1,0:T(8,128)}, f32[320,256]{1,0:T(8,128)}) custom-call(bf16[2048,4096]{1,0:T(8,128)(2,1)} %refs_0_.1, bf16[320,4096]{1,0:T(8,128)(2,1)} %bitcast.3), custom_call_target="tpu_custom_call" | custom-call | flops 10737418240 | bytes 25165824 | tf_op jit(solution)/shard_map/range_finder/pallas_call | solution.py:411
  59.3 0.0 copy-start
  59.3 3.6 %copy.6 = f32[2048,320]{0,1:T(8,128)} copy(f32[2048,320]{0,1:T(8,128)} %bitcast.2) | data formatting | bytes 5242880
  62.9 0.0 copy-done
  62.9 0.7 %copy.7 = f32[320,256]{1,0:T(8,128)} copy(f32[320,256]{1,0:T(8,128)S(1)} %copy-done) | data formatting | bytes 655360
Async XLA Ops:
  59.3 3.6 %copy-start = (f32[320,256]{1,0:T(8,128)S(1)}, f32[320,256]{1,0:T(8,128)}, u32[]{:S(2)}) copy-start(f32[320,256]{1,0:T(8,128)} %get-tuple-element.9) | copy-start | bytes 983044

commit v7 on v6

--- a/solution.py
+++ b/solution.py
@@ -20,6 +20,7 @@
 LOCAL = 2048
 CHUNK = 512
 STEP = 1024
+HAND = 8
 WIDTH = 256
 SLICES = 16
 SIDE = 4
@@ -37,7 +38,8 @@
 def dot3(a, b, dims):
     ah, al = split(a)
     bh, bl = split(b)
-    return dot(ah, bh, dims) + (dot(ah, bl, dims) + dot(al, bh, dims))
+    (ca,), (cb,) = dims[0]
+    return dot(jnp.concatenate([ah, al, ah], axis=ca), jnp.concatenate([bh, bh, bl], axis=cb), dims)
 
 
 def factor_block(a, n, w):
@@ -414,7 +416,7 @@
             jax.ShapeDtypeStruct((SK, LOCAL), F32),
             jax.ShapeDtypeStruct((SK, WIDTH), F32),
         ),
-        in_specs=[pl.BlockSpec(memory_space=pl.ANY)] * 2,
+        in_specs=[pl.BlockSpec(memory_space=pltpu.HBM)] * 2,
         out_specs=(
             pl.BlockSpec(memory_space=pl.ANY),
             pl.BlockSpec(memory_space=pltpu.VMEM),
@@ -450,7 +452,7 @@
             dma((2 * SIDE,)), dma((2 * SIDE,)),
         ],
         compiler_params=pltpu.CompilerParams(
-            collective_id=0, has_side_effects=True, vmem_limit_bytes=58 << 20
+            collective_id=0, has_side_effects=True, vmem_limit_bytes=50 << 20
         ),
         cost_estimate=pl.CostEstimate(
             flops=4 * LOCAL * N * SK, bytes_accessed=24 << 20, transcendentals=0
@@ -459,10 +461,42 @@
     )(slab, map_rows)
 
 
+def hand_over_kernel(basis_in, coeffs_in, basis_t, coeffs, sem):
+    rows = SK // HAND
+
+    def store(i):
+        part = pl.ds(i * rows, rows)
+        return pltpu.make_async_copy(basis_in.at[part], basis_t.at[part], sem.at[i])
+
+    copies = [store(i) for i in range(HAND)]
+    copies.append(pltpu.make_async_copy(coeffs_in, coeffs, sem.at[HAND]))
+    for copy in copies:
+        copy.start()
+    for copy in copies:
+        copy.wait()
+
+
+def hand_over(basis_t, coeffs):
+    vmem = pl.BlockSpec(memory_space=pltpu.VMEM)
+    hbm = pl.BlockSpec(memory_space=pltpu.HBM)
+    return pl.pallas_call(
+        hand_over_kernel,
+        out_shape=(
+            jax.ShapeDtypeStruct((SK, LOCAL), F32),
+            jax.ShapeDtypeStruct((SK, WIDTH), F32),
+        ),
+        in_specs=[vmem, vmem],
+        out_specs=(hbm, hbm),
+        scratch_shapes=[pltpu.SemaphoreType.DMA((HAND + 1,))],
+        compiler_params=pltpu.CompilerParams(vmem_limit_bytes=16 << 20),
+        name="hand_over",
+    )(basis_t, coeffs)
+
+
 def local(slab, sketch_map):
     rows = slab.shape[0] * lax.axis_size("grp") * lax.axis_size("dev")
     scale = math.sqrt(rows)
-    basis_t, coeffs = whole_call(scale, slab, sketch_map.T)
+    basis_t, coeffs = hand_over(*whole_call(scale, slab, sketch_map.T))
     return basis_t.T, coeffs
 
 

time: 63.8 us -> 60.2 us (0.944)
  local copies, waits for them, and re-layouts: 4.31 us -> 0 us
    unnamed x4 -> x0, local copies, waits for them, and re-layouts: 4.31 us -> none
    pallas_call x0 -> x1, Pallas kernels: none -> 1.67 us  [hand_over(): pl.pallas_call(hand_over_kernel, out_shape=(jax.ShapeDtypeStruct((SK, LOC...]
    pallas_call x1, Pallas kernels: 58.7 us -> 57.6 us  [whole_call(): pl.pallas_call(kernel, out_shape=(jax.ShapeDtypeStruct((SK, LOCAL), F32),...]
where the time goes in v7:
time: 60.2 us; the launch traced here: 60.1 us
  Pallas kernels  59.3 us (99%)
  between operations  0.8 us (1%)
    pallas_call x1, Pallas kernels, whole_call(): pl.pallas_call(kernel, out_shape=(jax.ShapeDtypeStruct((SK, LOCAL), F32),...  57.6 us
    pallas_call x1, Pallas kernels, hand_over(): pl.pallas_call(hand_over_kernel, out_shape=(jax.ShapeDtypeStruct((SK, LOC...  1.67 us

profile of v7, /device:TPU:1, one launch (start us, length us, event | category | flops | bytes accessed | tf_op | source)
XLA Modules:
  0.0 60.1 jit_solution(1087424827443667034)
XLA Ops:
  0.6 57.6 %range_finder.1 = (f32[320,2048]{1,0:T(8,128)S(1)}, f32[320,256]{1,0:T(8,128)S(1)}) custom-call(bf16[2048,4096]{1,0:T(8,128)(2,1)} %refs_0_.1, bf16[320,4096]{1,0:T(8,128)(2,1)} %bitcast.2), custom_call_target="tpu_custom_call" | custom-call | flops 10737418240 | bytes 25165824 | tf_op jit(solution)/shard_map/range_finder/pallas_call | solution.py:413
  58.3 1.7 %hand_over.1 = (f32[320,2048]{1,0:T(8,128)}, f32[320,256]{1,0:T(8,128)}) custom-call(f32[320,2048]{1,0:T(8,128)S(1)} %get-tuple-element.6.basis_in, f32[320,256]{1,0:T(8,128)S(1)} %get-tuple-element.7.coeffs_in), custom_call_target="tpu_custom_call" | custom-call | tf_op jit(solution)/shard_map/hand_over/pallas_call | solution.py:482

commit v8 on v7

--- a/solution.py
+++ b/solution.py
@@ -308,28 +308,28 @@
     for p in range(12, 16):
         add_core(p)
     a_copy(3).start()
-    for p in range(4):
-        add_core(p)
-
-    for i in (1, 3, 2):
-        g2(i).wait()
-    gtot[part] = (gline[0] + gline[1]) + (gline[2] + gline[3])
-
-    def g3(flip, dz, dx):
-        k = flip * SLICES + dz * SIDE + dx
-        to_g = other if flip else g
-        return remote(gtot.at[part], gtot.at[part], g3s.at[k], g3r.at[k], to_g, chip(dz, dx))
-
-    handed = [(flip, dz, dx) for dz, dx in AROUND for flip in (0, 1)] + [(1, 0, 0)]
-    for p in handed:
-        g3(*p).start()
-
     a_copy(0).wait()
     a_copy(1).wait()
     cross[4:6, mine, :] += from_a[0]
     cross[14:16, mine, :] += from_a[1]
     a_copy(4).start()
     a_copy(5).start()
+    for p in range(4):
+        add_core(p)
+
+    for i in (1, 3, 2):
+        g2(i).wait()
+    gtot[part] = (gline[0] + gline[1]) + (gline[2] + gline[3])
+
+    def g3(flip, dz, dx):
+        k = flip * SLICES + dz * SIDE + dx
+        to_g = other if flip else g
+        return remote(gtot.at[part], gtot.at[part], g3s.at[k], g3r.at[k], to_g, chip(dz, dx))
+
+    handed = [(flip, dz, dx) for dz, dx in AROUND for flip in (0, 1)] + [(1, 0, 0)]
+    for p in handed:
+        g3(*p).start()
+
     m[...] = jnp.zeros_like(m)
 
     for k in range(2, 6):

time: 60.2 us -> 59 us (0.980)
  Pallas kernels: 59.3 us -> 58 us
    pallas_call x1, Pallas kernels: 57.6 us -> 56.4 us  [whole_call(): pl.pallas_call(kernel, out_shape=(jax.ShapeDtypeStruct((SK, LOCAL), F32),...]
where the time goes in v8:
time: 59 us; the launch traced here: 58.8 us
  Pallas kernels  58 us (98%)
  between operations  0.8 us (1%)
    pallas_call x1, Pallas kernels, whole_call(): pl.pallas_call(kernel, out_shape=(jax.ShapeDtypeStruct((SK, LOCAL), F32),...  56.4 us
    pallas_call x1, Pallas kernels, hand_over(): pl.pallas_call(hand_over_kernel, out_shape=(jax.ShapeDtypeStruct((SK, LOC...  1.67 us

profile of v8, /device:TPU:1, one launch (start us, length us, event | category | flops | bytes accessed | tf_op | source)
XLA Modules:
  0.0 58.8 jit_solution(5463644088476488051)
XLA Ops:
  0.6 56.4 %range_finder.1 = (f32[320,2048]{1,0:T(8,128)S(1)}, f32[320,256]{1,0:T(8,128)S(1)}) custom-call(bf16[2048,4096]{1,0:T(8,128)(2,1)} %refs_0_.1, bf16[320,4096]{1,0:T(8,128)(2,1)} %bitcast.2), custom_call_target="tpu_custom_call" | custom-call | flops 10737418240 | bytes 25165824 | tf_op jit(solution)/shard_map/range_finder/pallas_call | solution.py:413
  57.0 1.7 %hand_over.1 = (f32[320,2048]{1,0:T(8,128)}, f32[320,256]{1,0:T(8,128)}) custom-call(f32[320,2048]{1,0:T(8,128)S(1)} %get-tuple-element.6.basis_in, f32[320,256]{1,0:T(8,128)S(1)} %get-tuple-element.7.coeffs_in), custom_call_target="tpu_custom_call" | custom-call | tf_op jit(solution)/shard_map/hand_over/pallas_call | solution.py:482

commit v9 on v8

--- a/solution.py
+++ b/solution.py
@@ -289,6 +289,10 @@
         add_core(p)
     a_copy(2).start()
     run_cross(12, 16)
+    cross_arrived(12, 16)
+    for p in range(12, 16):
+        add_core(p)
+    a_copy(3).start()
 
     for p in AROUND[::-1]:
         g1(*p).wait()
@@ -304,10 +308,6 @@
     for i in (2, 1, 3):
         g2(i).start()
 
-    cross_arrived(12, 16)
-    for p in range(12, 16):
-        add_core(p)
-    a_copy(3).start()
     a_copy(0).wait()
     a_copy(1).wait()
     cross[4:6, mine, :] += from_a[0]

time: 59 us -> 59 us (level)
  no operation moved by 1% of the time
where the time goes in v9:
time: 59 us; the launch traced here: 58.8 us
  Pallas kernels  58 us (98%)
  between operations  0.8 us (1%)
    pallas_call x1, Pallas kernels, whole_call(): pl.pallas_call(kernel, out_shape=(jax.ShapeDtypeStruct((SK, LOCAL), F32),...  56.4 us
    pallas_call x1, Pallas kernels, hand_over(): pl.pallas_call(hand_over_kernel, out_shape=(jax.ShapeDtypeStruct((SK, LOC...  1.67 us

profile of v9, /device:TPU:1, one launch (start us, length us, event | category | flops | bytes accessed | tf_op | source)
XLA Modules:
  0.0 58.8 jit_solution(15618548126722205826)
XLA Ops:
  0.6 56.4 %range_finder.1 = (f32[320,2048]{1,0:T(8,128)S(1)}, f32[320,256]{1,0:T(8,128)S(1)}) custom-call(bf16[2048,4096]{1,0:T(8,128)(2,1)} %refs_0_.1, bf16[320,4096]{1,0:T(8,128)(2,1)} %bitcast.2), custom_call_target="tpu_custom_call" | custom-call | flops 10737418240 | bytes 25165824 | tf_op jit(solution)/shard_map/range_finder/pallas_call | solution.py:413
  57.0 1.7 %hand_over.1 = (f32[320,2048]{1,0:T(8,128)}, f32[320,256]{1,0:T(8,128)}) custom-call(f32[320,2048]{1,0:T(8,128)S(1)} %get-tuple-element.6.basis_in, f32[320,256]{1,0:T(8,128)S(1)} %get-tuple-element.7.coeffs_in), custom_call_target="tpu_custom_call" | custom-call | tf_op jit(solution)/shard_map/hand_over/pallas_call | solution.py:482
